TPU v7x, 32 devices: a whole 2x2x4 slice. The times are simulated.
32 devices in a mesh: dp: 8 (over z, core), fsdp: 4 (over y, x).
Axes of the slice: x: 2, y: 2, z: 4, core: 2. Of those that a mesh axis runs over, the one named last changes fastest.
Arguments:
- frames: bfloat16 [32, 512, 1024], P(('dp', 'fsdp'))
- lengths: int32 [32], P(('dp', 'fsdp')), may hold values from 1 to 512, 12288 in all
- cotangent: bfloat16 [32, 512, 1024], P(('dp', 'fsdp')), may hold values from -6 to 6
- early_up: bfloat16 [1024, 4096], P('fsdp'), may hold values from -0.1875 to 0.1875
- early_down: bfloat16 [4096, 1024], P('fsdp'), may hold values from -0.09375 to 0.09375
- heads_in: bfloat16 [1024, 3072], P('fsdp'), may hold values from -0.1875 to 0.1875
- offset_proj: bfloat16 [1024, 1024], P('fsdp'), may hold values from -0.1875 to 0.1875
- heads_out: bfloat16 [1024, 1024], P('fsdp'), may hold values from -1 to 1
- pointwise_up: bfloat16 [1024, 2048], P('fsdp'), may hold values from -0.1875 to 0.1875
- pointwise_down: bfloat16 [1024, 1024], P('fsdp'), may hold values from -0.1875 to 0.1875
- late_up: bfloat16 [1024, 4096], P('fsdp'), may hold values from -0.1875 to 0.1875
- late_down: bfloat16 [4096, 1024], P('fsdp'), may hold values from -0.09375 to 0.09375
- depthwise: bfloat16 [5, 1024], P(None, 'fsdp'), may hold values from -2.5 to 2.5
- norm_gains: bfloat16 [6, 1024], P(None, 'fsdp'), may hold values from 0.5 to 1.5
- norm_shifts: bfloat16 [6, 1024], P(None, 'fsdp'), may hold values from -1.5 to 1.5
- score_bias: bfloat16 [2, 1024], P(None, 'fsdp'), may hold values from -3 to 3
Outputs:
- output: bfloat16 [32, 512, 1024], P(('dp', 'fsdp'))
- frames_grad: float32 [32, 512, 1024], P(('dp', 'fsdp'))
- early_up_grad: float32 [1024, 4096], P('fsdp')
- early_down_grad: float32 [4096, 1024], P('fsdp')
- heads_in_grad: float32 [1024, 3072], P('fsdp')
- offset_proj_grad: float32 [1024, 1024], P('fsdp')
- heads_out_grad: float32 [1024, 1024], P('fsdp')
- pointwise_up_grad: float32 [1024, 2048], P('fsdp')
- pointwise_down_grad: float32 [1024, 1024], P('fsdp')
- late_up_grad: float32 [1024, 4096], P('fsdp')
- late_down_grad: float32 [4096, 1024], P('fsdp')
- depthwise_grad: float32 [5, 1024], P(None, 'fsdp')
- norm_gains_grad: float32 [6, 1024], P(None, 'fsdp')
- norm_shifts_grad: float32 [6, 1024], P(None, 'fsdp')
- score_bias_grad: float32 [2, 1024], P(None, 'fsdp')
Inputs may be any that keep to these rules, and one draw needn't show every extreme that they name: `lengths`: each item has 1 to 512 valid frames at its start; some item has exactly 512.
All inputs are finite; a program needn't handle non-finite values. No bound on the sum of `lengths` on one device may be relied on, other than what follows from the above.
Results may differ from a plain program's by a relative error of at most 0.03.
Values may be sent and summed in bfloat16 or wider, within the bound.
A program may use at most 320 MiB of HBM per device.

v0:
```python
import math

import jax
import jax.numpy as jnp
from jax import lax
from jax.sharding import PartitionSpec as P

HEADS = 8


EPS = 1e-05


def product(left, right):
    return jnp.dot(left, right, preferred_element_type=jnp.float32)


def product_nt(left, right):
    return lax.dot_general(
        left, right, (((1,), (1,)), ((), ())), preferred_element_type=jnp.float32
    )


def product_tn(left, right):
    return lax.dot_general(
        left, right, (((0,), (0,)), ((), ())), preferred_element_type=jnp.float32
    )


def layer_norm(values, gain, shift):
    center = values - jnp.mean(values, axis=-1, keepdims=True)
    spread = jnp.mean(center * center, axis=-1, keepdims=True)
    return center * lax.rsqrt(spread + EPS) * gain + shift


def position_table(span, width):
    rows = jnp.arange(2 * span - 1)
    distance = (span - 1 - rows).astype(jnp.float32)
    columns = jnp.arange(width // 2).astype(jnp.float32)
    rate = jnp.exp(columns * (-2.0 * math.log(10000.0) / width))
    angle = distance[:, None] * rate[None, :]
    return jnp.concatenate([jnp.sin(angle), jnp.cos(angle)], axis=1)


def rel_shift(placed):
    lead = placed.shape[:-2]
    span = placed.shape[-2]
    padded = jnp.pad(placed, [(0, 0)] * (placed.ndim - 1) + [(0, 1)])
    flat = padded.reshape(lead + (2 * span * span,))
    flat = flat[..., span - 1 : span - 1 + span * (2 * span - 1)]
    return flat.reshape(lead + (span, 2 * span - 1))[..., :span]


def rel_unshift(grads):
    lead = grads.shape[:-2]
    span = grads.shape[-1]
    wide = jnp.pad(grads, [(0, 0)] * (grads.ndim - 1) + [(0, span - 1)])
    flat = wide.reshape(lead + (span * (2 * span - 1),))
    flat = jnp.pad(flat, [(0, 0)] * len(lead) + [(span - 1, 1)])
    return flat.reshape(lead + (span, 2 * span))[..., : 2 * span - 1]


def fetch(first, second):
    return (
        lax.all_gather(first, "fsdp", axis=0, tiled=True),
        lax.all_gather(second, "fsdp", axis=0, tiled=True),
    )


def fetch_again(first, second):
    return (
        lax.all_gather(first, "fsdp", axis=0, tiled=True),
        lax.all_gather(second, "fsdp", axis=0, tiled=True),
    )


def reduce_pair(first, second):
    shards = (
        lax.psum_scatter(
            first.astype(jnp.bfloat16), "fsdp", scatter_dimension=0, tiled=True
        ).astype(jnp.float32),
        lax.psum_scatter(
            second.astype(jnp.bfloat16), "fsdp", scatter_dimension=0, tiled=True
        ).astype(jnp.float32),
    )
    return (
        lax.psum(shards[0].astype(jnp.bfloat16), "dp").astype(jnp.float32),
        lax.psum(shards[1].astype(jnp.bfloat16), "dp").astype(jnp.float32),
    )


def feed_forward(state, up_proj, down_proj, gain, shift):
    width = state.shape[-1]
    flat = state.reshape(-1, width)
    hidden = layer_norm(flat, gain, shift).astype(jnp.bfloat16)
    inner = product(hidden, up_proj)
    active = jax.nn.silu(inner).astype(jnp.bfloat16)
    return (state + 0.5 * product(active, down_proj).reshape(state.shape), hidden, inner, active)


def feed_forward_back(state, grad, up_proj, down_proj, gain, shift):
    width = state.shape[-1]
    _, hidden, inner, active = feed_forward(state, up_proj, down_proj, gain, shift)
    branch = (0.5 * grad.reshape(-1, width)).astype(jnp.bfloat16)
    down_grad = product_tn(active, branch)
    active_grad = product_nt(branch, down_proj)
    inner_grad = jax.vjp(jax.nn.silu, inner)[1](active_grad)[0].astype(jnp.bfloat16)
    up_grad = product_tn(hidden, inner_grad)
    hidden_grad = product_nt(inner_grad, up_proj)
    _, norm_back = jax.vjp(layer_norm, state.reshape(-1, width), gain, shift)
    state_grad, gain_grad, shift_grad = norm_back(hidden_grad)
    return (grad + state_grad.reshape(grad.shape), up_grad, down_grad, gain_grad, shift_grad)


def attention_forward(state, valid, heads_in, offset_proj, score_bias, gain, shift, table, heads):
    items, span, width = state.shape
    head_size = width // heads
    flat = state.reshape(items * span, width)
    hidden = layer_norm(flat, gain, shift).astype(jnp.bfloat16)
    joint = product(hidden, heads_in)
    query = joint[:, :width]
    keys = joint[:, width : 2 * width].astype(jnp.bfloat16).reshape(items, span, heads, head_size)
    values = joint[:, 2 * width :].astype(jnp.bfloat16).reshape(items, span, heads, head_size)
    query_content = (
        (query + score_bias[0]).astype(jnp.bfloat16).reshape(items, span, heads, head_size)
    )
    query_offset = (
        (query + score_bias[1]).astype(jnp.bfloat16).reshape(items, span, heads, head_size)
    )
    offsets = (
        product(table, offset_proj).astype(jnp.bfloat16).reshape(2 * span - 1, heads, head_size)
    )
    content = jnp.einsum("ishe,ithe->ihst", query_content, keys, preferred_element_type=jnp.float32)
    placed = jnp.einsum("ishe,mhe->ihsm", query_offset, offsets, preferred_element_type=jnp.float32)
    raw = content + rel_shift(placed)
    scores = jnp.where(valid[:, None, None, :] > 0.5, raw * head_size ** (-0.5), -1e30)
    weights = jax.nn.softmax(scores, axis=-1)
    probs = weights.astype(jnp.bfloat16)
    mixed = jnp.einsum("ihst,ithe->ishe", probs, values, preferred_element_type=jnp.float32)
    mixed = mixed.reshape(items * span, width).astype(jnp.bfloat16)
    return (hidden, keys, values, query_content, query_offset, offsets, weights, probs, mixed)


def attention_back(
    state, grad, valid, heads_in, offset_proj, heads_out, score_bias, gain, shift, table, heads
):
    items, span, width = state.shape
    head_size = width // heads
    hidden, keys, values, query_content, query_offset, offsets, weights, probs, mixed = (
        attention_forward(
            state, valid, heads_in, offset_proj, score_bias, gain, shift, table, heads
        )
    )
    out_grad = grad.reshape(items * span, width).astype(jnp.bfloat16)
    heads_out_grad = product_tn(mixed, out_grad)
    mixed_grad = (
        product_nt(out_grad, heads_out).astype(jnp.bfloat16).reshape(items, span, heads, head_size)
    )
    prob_grad = jnp.einsum(
        "ishe,ithe->ihst", mixed_grad, values, preferred_element_type=jnp.float32
    )
    values_grad = jnp.einsum(
        "ihst,ishe->ithe", probs, mixed_grad, preferred_element_type=jnp.float32
    )
    score_grad = weights * (prob_grad - jnp.sum(weights * prob_grad, axis=-1, keepdims=True))
    raw_grad = (score_grad * head_size ** (-0.5)).astype(jnp.bfloat16)
    content_grad = jnp.einsum("ihst,ithe->ishe", raw_grad, keys, preferred_element_type=jnp.float32)
    keys_grad = jnp.einsum(
        "ihst,ishe->ithe", raw_grad, query_content, preferred_element_type=jnp.float32
    )
    placed_grad = rel_unshift(raw_grad)
    offset_grad = jnp.einsum(
        "ihsm,mhe->ishe", placed_grad, offsets, preferred_element_type=jnp.float32
    )
    offsets_grad = jnp.einsum(
        "ihsm,ishe->mhe", placed_grad, query_offset, preferred_element_type=jnp.float32
    )
    offsets_grad = offsets_grad.reshape(2 * span - 1, width).astype(jnp.bfloat16)
    offset_proj_grad = product_tn(table, offsets_grad)
    content_grad = content_grad.reshape(items * span, width)
    offset_grad = offset_grad.reshape(items * span, width)
    bias_grad = jnp.stack([jnp.sum(content_grad, axis=0), jnp.sum(offset_grad, axis=0)])
    joint_grad = jnp.concatenate(
        [
            content_grad + offset_grad,
            keys_grad.reshape(items * span, width),
            values_grad.reshape(items * span, width),
        ],
        axis=1,
    ).astype(jnp.bfloat16)
    heads_in_grad = product_tn(hidden, joint_grad)
    hidden_grad = product_nt(joint_grad, heads_in)
    _, norm_back = jax.vjp(layer_norm, state.reshape(-1, width), gain, shift)
    state_grad, gain_grad, shift_grad = norm_back(hidden_grad)
    return (
        grad + state_grad.reshape(state.shape),
        heads_in_grad,
        offset_proj_grad,
        heads_out_grad,
        bias_grad,
        gain_grad,
        shift_grad,
    )


def glu_conv(lifted, kernel, valid):
    items, span = valid.shape
    width = kernel.shape[1]
    gated = lifted[:, :width] * jax.nn.sigmoid(lifted[:, width:])
    gated = gated.reshape(items, span, width) * valid[:, :, None]
    half = kernel.shape[0] // 2
    padded = jnp.pad(gated, ((0, 0), (half, half), (0, 0)))
    total = jnp.zeros_like(gated)
    for index in range(kernel.shape[0]):
        total = total + kernel[index] * padded[:, index : index + span]
    return total


def conv_front(state, valid, pointwise_up, kernel, gain, shift):
    flat = state.reshape(-1, state.shape[-1])
    hidden = layer_norm(flat, gain, shift).astype(jnp.bfloat16)
    lifted = product(hidden, pointwise_up)
    return (hidden, lifted, glu_conv(lifted, kernel, valid))


def conv_rest(convolved, mean, inverse, gain, shift):
    normal = (convolved - mean) * inverse
    scaled = normal * gain + shift
    swished = jax.nn.silu(scaled).reshape(-1, convolved.shape[-1]).astype(jnp.bfloat16)
    return (normal, scaled, swished)


def body(
    frames,
    lengths,
    cotangent,
    early_up,
    early_down,
    heads_in,
    offset_proj,
    heads_out,
    pointwise_up,
    pointwise_down,
    late_up,
    late_down,
    depthwise,
    norm_gains,
    norm_shifts,
    score_bias,
):
    items, span, width = frames.shape
    taps = depthwise.shape[0]
    valid = (lax.broadcasted_iota(jnp.int32, (items, span), 1) < lengths[:, None]).astype(
        jnp.float32
    )
    mask = valid[:, :, None]
    table = position_table(span, width).astype(jnp.bfloat16)
    start = frames.astype(jnp.float32)
    small = jnp.concatenate([norm_gains.T, norm_shifts.T, score_bias.T, depthwise.T], axis=1)
    small_full, early_up_full = fetch(small, early_up)
    small_wide = small_full.astype(jnp.float32)
    gains = small_wide[:, 0:6].T
    shifts = small_wide[:, 6:12].T
    bias_full = small_wide[:, 12:14].T
    kernel = small_wide[:, 14 : 14 + taps].T
    early_down_full, heads_in_full = fetch(early_down, heads_in)
    after_early = feed_forward(start, early_up_full, early_down_full, gains[0], shifts[0])[0]
    offset_full, heads_out_full = fetch(offset_proj, heads_out)
    parts = attention_forward(
        after_early, valid, heads_in_full, offset_full, bias_full, gains[1], shifts[1], table, HEADS
    )
    after_attention = after_early + product(parts[8], heads_out_full).reshape(frames.shape)
    conv_up_full, conv_down_full = fetch(pointwise_up, pointwise_down)
    hidden_conv, lifted, convolved = conv_front(
        after_attention, valid, conv_up_full, kernel, gains[2], shifts[2]
    )
    local = (
        jnp.sum(convolved * mask, axis=(0, 1)),
        jnp.sum(convolved * convolved * mask, axis=(0, 1)),
        jnp.sum(valid),
    )
    sums, squares, count = lax.psum((local[0], local[1], local[2]), ("dp", "fsdp"))
    mean = sums / count
    inverse = lax.rsqrt(squares / count - mean * mean + EPS)
    normal, scaled, swished = conv_rest(convolved, mean, inverse, gains[5], shifts[5])
    after_conv = after_attention + product(swished, conv_down_full).reshape(frames.shape)
    late_up_full, late_down_full = fetch(late_up, late_down)
    after_late = feed_forward(after_conv, late_up_full, late_down_full, gains[3], shifts[3])[0]
    output = (layer_norm(after_late, gains[4], shifts[4]) * mask).astype(jnp.bfloat16)
    final_grad = cotangent.astype(jnp.float32) * mask
    _, final_back = jax.vjp(layer_norm, after_late, gains[4], shifts[4])
    grad, gain_final, shift_final = final_back(final_grad)
    late_up_full, late_down_full = fetch_again(late_up, late_down)
    grad, late_up_grad, late_down_grad, gain_late, shift_late = feed_forward_back(
        after_conv, grad, late_up_full, late_down_full, gains[3], shifts[3]
    )
    late_shards = reduce_pair(late_up_grad, late_down_grad)
    conv_up_full, conv_down_full = fetch_again(pointwise_up, pointwise_down)
    hidden_conv, lifted, convolved = conv_front(
        after_attention, valid, conv_up_full, kernel, gains[2], shifts[2]
    )
    normal, scaled, swished = conv_rest(convolved, mean, inverse, gains[5], shifts[5])
    out_grad = grad.reshape(-1, width).astype(jnp.bfloat16)
    pointwise_down_grad = product_tn(swished, out_grad)
    swish_grad = product_nt(out_grad, conv_down_full).reshape(frames.shape)
    scaled_grad = jax.vjp(jax.nn.silu, scaled)[1](swish_grad)[0]
    local_back = (
        jnp.sum(scaled_grad * mask, axis=(0, 1)),
        jnp.sum(scaled_grad * normal * mask, axis=(0, 1)),
    )
    shift_total, gain_total = lax.psum((local_back[0], local_back[1]), ("dp", "fsdp"))
    conv_grad = (
        inverse * gains[5] * (scaled_grad - mask * (shift_total + normal * gain_total) / count)
    )
    _, glu_back = jax.vjp(
        lambda lifted_in, kernel_in: glu_conv(lifted_in, kernel_in, valid), lifted, kernel
    )
    lifted_grad, kernel_grad = glu_back(conv_grad)
    lifted_grad = lifted_grad.astype(jnp.bfloat16)
    pointwise_up_grad = product_tn(hidden_conv, lifted_grad)
    hidden_grad = product_nt(lifted_grad, conv_up_full)
    _, conv_norm_back = jax.vjp(layer_norm, after_attention.reshape(-1, width), gains[2], shifts[2])
    state_grad, gain_conv, shift_conv = conv_norm_back(hidden_grad)
    grad = grad + state_grad.reshape(frames.shape)
    conv_shards = reduce_pair(pointwise_up_grad, pointwise_down_grad)
    offset_full, heads_out_full = fetch_again(offset_proj, heads_out)
    early_down_full, heads_in_full = fetch_again(early_down, heads_in)
    (
        grad,
        heads_in_grad,
        offset_proj_grad,
        heads_out_grad,
        bias_grad,
        gain_attention,
        shift_attention,
    ) = attention_back(
        after_early,
        grad,
        valid,
        heads_in_full,
        offset_full,
        heads_out_full,
        bias_full,
        gains[1],
        shifts[1],
        table,
        HEADS,
    )
    middle_shards = reduce_pair(offset_proj_grad, heads_out_grad)
    small_full, early_up_full = fetch_again(small, early_up)
    grad, early_up_grad, early_down_grad, gain_early, shift_early = feed_forward_back(
        start, grad, early_up_full, early_down_full, gains[0], shifts[0]
    )
    inner_shards = reduce_pair(early_down_grad, heads_in_grad)
    gains_grad = jnp.stack(
        [gain_early, gain_attention, gain_conv, gain_late, gain_final, local_back[1]]
    )
    shifts_grad = jnp.stack(
        [shift_early, shift_attention, shift_conv, shift_late, shift_final, local_back[0]]
    )
    small_grad = jnp.concatenate([gains_grad.T, shifts_grad.T, bias_grad.T, kernel_grad.T], axis=1)
    outer_shards = reduce_pair(small_grad, early_up_grad)
    small_shard = outer_shards[0]
    return (
        output,
        grad,
        outer_shards[1],
        inner_shards[0],
        inner_shards[1],
        middle_shards[0],
        middle_shards[1],
        conv_shards[0],
        conv_shards[1],
        late_shards[0],
        late_shards[1],
        small_shard[:, 14 : 14 + taps].T,
        small_shard[:, 0:6].T,
        small_shard[:, 6:12].T,
        small_shard[:, 12:14].T,
    )


def solution(mesh):
    in_specs = (
        P(("dp", "fsdp"), None, None),
        P(("dp", "fsdp")),
        P(("dp", "fsdp"), None, None),
        P("fsdp", None),
        P("fsdp", None),
        P("fsdp", None),
        P("fsdp", None),
        P("fsdp", None),
        P("fsdp", None),
        P("fsdp", None),
        P("fsdp", None),
        P("fsdp", None),
        P(None, "fsdp"),
        P(None, "fsdp"),
        P(None, "fsdp"),
        P(None, "fsdp"),
    )
    out_specs = (
        P(("dp", "fsdp"), None, None),
        P(("dp", "fsdp"), None, None),
        P("fsdp", None),
        P("fsdp", None),
        P("fsdp", None),
        P("fsdp", None),
        P("fsdp", None),
        P("fsdp", None),
        P("fsdp", None),
        P("fsdp", None),
        P("fsdp", None),
        P(None, "fsdp"),
        P(None, "fsdp"),
        P(None, "fsdp"),
        P(None, "fsdp"),
    )
    return jax.shard_map(body, mesh=mesh, in_specs=in_specs, out_specs=out_specs, check_vma=False)
```

profile of v0, /device:TPU:0, one launch (start us, length us, event | category | flops | bytes accessed | tf_op | source)
XLA Modules:
  0.0 1711.6 jit_solution(7839830453079510853)
XLA Ops:
  56.0 81.4 %all-gather.10.cloned.1.call-done = bf16[1024,4096]{1,0:T(8,128)(2,1)} async-done(((bf16[256,4096]{1,0:T(8,128)(2,1)}), bf16[1024,4096]{1,0:T(8,128)(2,1)}) %all-gather.10.cloned.1.call-update) | async-done | bytes 8388624 | tf_op jit(solution)/shard_map/all_gather | solution.py:66
  148.0 78.9 %all-gather.12.cloned.1.call-done = bf16[4096,1024]{1,0:T(8,128)(2,1)} async-done(((bf16[1024,1024]{1,0:T(8,128)(2,1)}), bf16[4096,1024]{1,0:T(8,128)(2,1)}) %all-gather.12.cloned.1.call-update) | async-done | bytes 8388624 | tf_op jit(solution)/shard_map/all_gather | solution.py:65
  238.2 60.6 %all-gather.14.cloned.1.call-done = bf16[1024,3072]{1,0:T(8,128)(2,1)} async-done(((bf16[256,3072]{1,0:T(8,128)(2,1)}), bf16[1024,3072]{1,0:T(8,128)(2,1)}) %all-gather.14.cloned.1.call-update) | async-done | bytes 6291472 | tf_op jit(solution)/shard_map/all_gather | solution.py:66
  319.1 16.4 copy.90
  347.6 14.5 reshape.544
  362.1 13.0 slice.216
  387.6 17.4 %reshape.545 = f32[1,8,512,1023]{3,2,1,0:T(8,128)} reshape(f32[4190208]{0:T(1024)} %reshape.572) | data formatting | bytes 33521664 | tf_op jit(solution)/shard_map/reshape | solution.py:51
  453.0 39.9 %all-reduce.17 = (f32[1024]{0:T(1024)S(1)}, f32[]{:T(128)}, f32[1024]{0:T(1024)S(1)}) all-reduce(f32[1024]{0:T(1024)S(1)} %get-tuple-element.33, f32[]{:T(128)} %fusion.89, f32[1024]{0:T(1024)S(1)} %get-tuple-element.32), channel_id=1, replica_groups=mesh['dp'=8,'fsdp'=4] {'dp','fsdp'}, use_global_device_ids=true, to_apply=%region_13.14 | all-reduce | flops 2049 | bytes 16392 | tf_op jit(solution)/shard_map/psum | solution.py:282
  499.7 18.5 %all-gather.24.cloned.1.call-done = bf16[1024,4096]{1,0:T(8,128)(2,1)} async-done(((bf16[256,4096]{1,0:T(8,128)(2,1)}), bf16[1024,4096]{1,0:T(8,128)(2,1)}) %all-gather.24.cloned.1.call-update) | async-done | bytes 8388624 | tf_op jit(solution)/shard_map/all_gather | solution.py:65
  518.3 12.8 fusion.115
  531.1 76.7 %all-gather.26.cloned.1.call-done = bf16[4096,1024]{1,0:T(8,128)(2,1)} async-done(((bf16[1024,1024]{1,0:T(8,128)(2,1)}), bf16[4096,1024]{1,0:T(8,128)(2,1)}) %all-gather.26.cloned.1.call-update) | async-done | bytes 8388624 | tf_op jit(solution)/shard_map/all_gather | solution.py:66
  623.5 13.6 fusion.2
  651.8 39.8 %all-reduce.16 = (f32[1024]{0:T(1024)S(1)}, f32[1024]{0:T(1024)S(1)}) all-reduce(f32[1024]{0:T(1024)S(1)} %get-tuple-element.31, f32[1024]{0:T(1024)S(1)} %get-tuple-element.30), channel_id=1, replica_groups=mesh['dp'=8,'fsdp'=4] {'dp','fsdp'}, use_global_device_ids=true, to_apply=%region_25.26 | all-reduce | flops 2048 | bytes 16384 | tf_op jit(solution)/shard_map/psum | solution.py:311
  740.0 14.0 reshape.574
  754.1 15.6 reshape.557
  922.0 45.0 %reduce-scatter.21.cloned.1.call-done = bf16[256,2048]{1,0:T(8,128)(2,1)} async-done(((bf16[1024,2048]{1,0:T(8,128)(2,1)}), bf16[256,2048]{1,0:T(8,128)(2,1)}) %reduce-scatter.21.cloned.1.call-update) | async-done | bytes 1048592 | tf_op jit(solution)/shard_map/reduce_scatter | solution.py:79
  967.0 73.1 %reduce-scatter.15.cloned.1.call-done = bf16[256,3072]{1,0:T(8,128)(2,1)} async-done(((bf16[1024,3072]{1,0:T(8,128)(2,1)}), bf16[256,3072]{1,0:T(8,128)(2,1)}) %reduce-scatter.15.cloned.1.call-update) | async-done | bytes 1572880 | tf_op jit(solution)/shard_map/reduce_scatter | solution.py:82
  1040.0 89.4 %reduce-scatter.11.cloned.1.call-done = bf16[256,4096]{1,0:T(8,128)(2,1)} async-done(((bf16[1024,4096]{1,0:T(8,128)(2,1)}), bf16[256,4096]{1,0:T(8,128)(2,1)}) %reduce-scatter.11.cloned.1.call-update) | async-done | bytes 2097168 | tf_op jit(solution)/shard_map/reduce_scatter | solution.py:82
  1129.4 89.6 %reduce-scatter.13.cloned.1.call-done = bf16[1024,1024]{1,0:T(8,128)(2,1)} async-done(((bf16[4096,1024]{1,0:T(8,128)(2,1)}), bf16[1024,1024]{1,0:T(8,128)(2,1)}) %reduce-scatter.13.cloned.1.call-update) | async-done | bytes 2097168 | tf_op jit(solution)/shard_map/reduce_scatter | solution.py:79
  1219.1 89.3 %reduce-scatter.25.cloned.1.call-done = bf16[256,4096]{1,0:T(8,128)(2,1)} async-done(((bf16[1024,4096]{1,0:T(8,128)(2,1)}), bf16[256,4096]{1,0:T(8,128)(2,1)}) %reduce-scatter.25.cloned.1.call-update) | async-done | bytes 2097168 | tf_op jit(solution)/shard_map/reduce_scatter | solution.py:79
  1308.4 89.7 %reduce-scatter.27.cloned.1.call-done = bf16[1024,1024]{1,0:T(8,128)(2,1)} async-done(((bf16[4096,1024]{1,0:T(8,128)(2,1)}), bf16[1024,1024]{1,0:T(8,128)(2,1)}) %reduce-scatter.27.cloned.1.call-update) | async-done | bytes 2097168 | tf_op jit(solution)/shard_map/reduce_scatter | solution.py:82
  1403.3 21.2 %reduce-scatter.29.cloned.1.call-done = bf16[256,19]{0,1:T(8,128)(2,1)} async-done(((bf16[1024,19]{0,1:T(8,128)(2,1)}), bf16[256,19]{0,1:T(8,128)(2,1)}) %reduce-scatter.29.cloned.1.call-update) | async-done | bytes 9744 | tf_op jit(solution)/shard_map/reduce_scatter | solution.py:79
  1424.5 28.7 %psum.119 = bf16[256,19]{0,1:T(8,128)(2,1)S(1)} all-reduce(bf16[256,19]{0,1:T(8,128)(2,1)} %reduce-scatter.29.cloned.1.call-done), channel_id=1, replica_groups=mesh['dp'=8,'fsdp'=4] {'dp'}, use_global_device_ids=true, to_apply=%region_69.70 | all-reduce | flops 4864 | bytes 19456 | tf_op jit(solution)/shard_map/psum | solution.py:87
  1455.0 230.8 %all-reduce.21.cloned.1.call-done = (bf16[256,4096]{1,0:T(8,128)(2,1)}, bf16[1024,1024]{1,0:T(8,128)(2,1)}, bf16[256,3072]{1,0:T(8,128)(2,1)}, bf16[256,1024]{1,...) async-done(((bf16[256,4096]{1,0:T(8,128)(2,1)}, ...) | async-done | bytes 12582928 | tf_op jit(solution)/shard_map/psum | solution.py:88
  (446 shorter events, 424.6 us)
Async XLA Ops:
  7.2 40.7 %all-gather.16.cloned.1.call-start = ((), (), s32[]{:S(2)}) async-start(), calls=%async_computation.13 | async-start | bytes 2621440 | tf_op jit(solution)/shard_map/all_gather | solution.py:65
  7.9 129.5 %all-gather.10.cloned.1.call-start = ((), (), s32[]{:S(2)}) async-start(), calls=%async_computation.10 | async-start | bytes 10485760 | tf_op jit(solution)/shard_map/all_gather | solution.py:66
  8.7 218.2 %all-gather.12.cloned.1.call-start = ((), (), s32[]{:S(2)}) async-start(), calls=%async_computation.11 | async-start | bytes 10485760 | tf_op jit(solution)/shard_map/all_gather | solution.py:65
  9.4 289.4 %all-gather.14.cloned.1.call-start = ((), (), s32[]{:S(2)}) async-start(), calls=%async_computation.12 | async-start | bytes 7864320 | tf_op jit(solution)/shard_map/all_gather | solution.py:66
  10.0 427.0 %all-gather.18.cloned.1.call-start = ((), (), s32[]{:S(2)}) async-start(), calls=%async_computation.14 | async-start | bytes 2621440 | tf_op jit(solution)/shard_map/all_gather | solution.py:66
  10.6 431.8 %all-gather.20.cloned.1.call-start = ((), (), s32[]{:S(2)}) async-start(), calls=%async_computation.15 | async-start | bytes 5242880 | tf_op jit(solution)/shard_map/all_gather | solution.py:65
  11.1 482.5 %all-gather.22.cloned.1.call-start = ((), (), s32[]{:S(2)}) async-start(), calls=%async_computation.16 | async-start | bytes 2621440 | tf_op jit(solution)/shard_map/all_gather | solution.py:66
  11.9 506.3 %all-gather.24.cloned.1.call-start = ((), (), s32[]{:S(2)}) async-start(), calls=%async_computation.17 | async-start | bytes 10485760 | tf_op jit(solution)/shard_map/all_gather | solution.py:65
  12.7 595.1 %all-gather.26.cloned.1.call-start = ((), (), s32[]{:S(2)}) async-start(), calls=%async_computation.18 | async-start | bytes 10485760 | tf_op jit(solution)/shard_map/all_gather | solution.py:66
  13.4 908.5 %reduce-scatter.17.cloned.1.call-start = ((), (), s32[]{:S(2)}) async-start(), calls=%async_computation.22 | async-start | bytes 2621440 | tf_op jit(solution)/shard_map/reduce_scatter | solution.py:79
  27.6 271.2 %copy-start.86 = (f32[1,1024]{1,0:T(1,128)}, f32[1,1024]{1,0:T(1,128)S(1)}, u32[]{:S(2)}) copy-start(f32[1,1024]{1,0:T(1,128)S(1)} %get-tuple-element.84) | copy-start | bytes 12292
  27.6 271.2 %copy-start.104 = (f32[1,1024]{1,0:T(1,128)}, f32[1,1024]{1,0:T(1,128)S(1)}, u32[]{:S(2)}) copy-start(f32[1,1024]{1,0:T(1,128)S(1)} %get-tuple-element.127) | copy-start | bytes 12292
  27.6 414.8 %copy-start.106 = (f32[1,1024]{1,0:T(1,128)}, f32[1,1024]{1,0:T(1,128)S(1)}, u32[]{:S(2)}) copy-start(f32[1,1024]{1,0:T(1,128)S(1)} %get-tuple-element.128) | copy-start | bytes 12292
  56.0 254.9 %copy-start.10 = (bf16[1023,1024]{0,1:T(8,128)(2,1)}, bf16[1023,1024]{0,1:T(8,128)(2,1)S(1)}, u32[]{:S(2)}) copy-start(bf16[1023,1024]{0,1:T(8,128)(2,1)S(1)} %copy.94) | copy-start | bytes 6285316
  797.8 124.1 %reduce-scatter.19.cloned.1.call-start = ((), (), s32[]{:S(2)}) async-start(), calls=%async_computation.23 | async-start | bytes 2621440 | tf_op jit(solution)/shard_map/reduce_scatter | solution.py:82
  803.2 118.8 %reduce-scatter.23.cloned.1.call-start = ((), (), s32[]{:S(2)}) async-start(), calls=%async_computation.25 | async-start | bytes 2621440 | tf_op jit(solution)/shard_map/reduce_scatter | solution.py:82
  808.5 158.5 %reduce-scatter.21.cloned.1.call-start = ((), (), s32[]{:S(2)}) async-start(), calls=%async_computation.24 | async-start | bytes 5242880 | tf_op jit(solution)/shard_map/reduce_scatter | solution.py:79
  816.1 223.9 %reduce-scatter.15.cloned.1.call-start = ((), (), s32[]{:S(2)}) async-start(), calls=%async_computation.21 | async-start | bytes 7864320 | tf_op jit(solution)/shard_map/reduce_scatter | solution.py:82
  842.4 287.0 %reduce-scatter.11.cloned.1.call-start = ((), (), s32[]{:S(2)}) async-start(), calls=%async_computation.19 | async-start | bytes 10485760 | tf_op jit(solution)/shard_map/reduce_scatter | solution.py:82
  874.0 345.0 %reduce-scatter.13.cloned.1.call-start = ((), (), s32[]{:S(2)}) async-start(), calls=%async_computation.20 | async-start | bytes 10485760 | tf_op jit(solution)/shard_map/reduce_scatter | solution.py:79
  885.2 423.2 %reduce-scatter.25.cloned.1.call-start = ((), (), s32[]{:S(2)}) async-start(), calls=%async_computation.26 | async-start | bytes 10485760 | tf_op jit(solution)/shard_map/reduce_scatter | solution.py:79
  896.2 501.9 %reduce-scatter.27.cloned.1.call-start = ((), (), s32[]{:S(2)}) async-start(), calls=%async_computation.27 | async-start | bytes 10485760 | tf_op jit(solution)/shard_map/reduce_scatter | solution.py:82
  908.9 515.6 %reduce-scatter.29.cloned.1.call-start = ((), (), s32[]{:S(2)}) async-start(), calls=%async_computation.28 | async-start | bytes 61440 | tf_op jit(solution)/shard_map/reduce_scatter | solution.py:79
  921.6 764.2 %all-reduce.21.cloned.1.call-start = ((), (), s32[]{:S(2)}) async-start(), calls=%async_computation.29 | async-start | bytes 25165824 | tf_op jit(solution)/shard_map/psum | solution.py:88
  (123 other events, 1677.3 us)
Sparse Core Ops, SparseCore 0:
  9.9 38.0 all-gather.15
  49.8 87.5 all-gather.9
  139.3 87.5 all-gather.11
  228.6 70.1 all-gather.13
  300.5 35.3 all-gather.17
  337.5 52.6 all-gather.19
  392.1 35.3 all-gather.21
  429.3 88.9 all-gather.23
  520.1 87.5 all-gather.25
  797.9 35.9 reduce-scatter.16
  837.2 35.2 reduce-scatter.18
  875.2 35.1 reduce-scatter.22
  914.2 52.6 reduce-scatter.20
  969.8 70.1 reduce-scatter.14
  1043.0 86.4 reduce-scatter.10
  1132.6 86.3 reduce-scatter.12
  1222.0 86.3 reduce-scatter.24
  1311.6 86.4 reduce-scatter.26
  1401.4 23.0 reduce-scatter.28
  1427.7 257.9 all-reduce.20
where the time goes:
time: 1720 us; the launch traced here: 1710 us
  waiting for transfers between devices  1060 us (62%)
  matrix products  238 us (14%)
  local copies, waits for them, and re-layouts  212 us (12%)
  blocking collectives  119 us (7%)
  other arithmetic  62.6 us (4%)
    reduce_scatter x5, waiting for transfers between devices, reduce_pair(): lax.psum_scatter(second.astype(jnp.bfloat16), 'fsdp', scatter_dimension=0...  252 us
    reduce_scatter x5, waiting for transfers between devices, reduce_pair(): lax.psum_scatter(first.astype(jnp.bfloat16), 'fsdp', scatter_dimension=0,...  245 us
    psum x1, waiting for transfers between devices, reduce_pair(): lax.psum(shards[1].astype(jnp.bfloat16), 'dp').astype(jnp.float32)  231 us
    all_gather x5, waiting for transfers between devices, fetch(): lax.all_gather(second, 'fsdp', axis=0, tiled=True)  219 us
    all_gather x4, waiting for transfers between devices, fetch(): lax.all_gather(first, 'fsdp', axis=0, tiled=True)  110 us
    unnamed x262, local copies, waits for them, and re-layouts  103 us
    dot_general x9, matrix products, product(): return jnp.dot(left, right, preferred_element_type=jnp.float32)  70.9 us
    dot_general x9, matrix products, product_tn(): lax.dot_general(left, right, (((0,), (0,)), ((), ())), preferred_element_...  67.6 us
  transfers between devices with their start and end apart: 20, of which 14 were waited for; matrix products, arithmetic and copies ran while one was open for 19% of the time, Pallas kernels for 0%

commit v1 on v0

v1 whole, which is shorter than its diff:
```python
import functools
import math
import types

import jax
import jax.numpy as jnp
import numpy as np
from jax import lax
from jax.experimental import pallas as pl
from jax.experimental.pallas import tpu as pltpu
from jax.sharding import PartitionSpec as P

MESH = pl.DeviceIdType.MESH


def flip(index, bit):
    return index + bit - 2 * bit * ((index // bit) % 2)


def bits_of(count):
    bits, bit = [], 1
    while bit < count:
        bits.append(bit)
        bit *= 2
    return bits


def span_of(bits):
    held = [0]
    for bit in bits:
        held = held + [h + bit for h in held]
    return held


def flips(index, mask):
    bit = 1
    while bit <= mask:
        if mask & bit:
            index = flip(index, bit)
        bit *= 2
    return index


def gather_items(shapes):
    items = []
    for w, (rows, cols) in enumerate(shapes):
        half = rows // 2
        row_step = min(half, 128 if w == len(shapes) - 1 else 256)
        col_step = cols if cols <= 2048 else (2048 if cols % 2048 == 0 else 1536)
        for row in range(0, half, row_step):
            for col in range(0, cols, col_step):
                tiles = col_step // 128
                side = tiles // 3
                if tiles % 3 == 2 and len(items) % 2:
                    side += 1
                items.append((w, row, row_step, col, side * 128, (tiles - 2 * side) * 128))
    return items


UR = 128


def unit_cols(count):
    return 2048 // count

LAG = 2
RING = 2 * LAG + 2
ZRING = 6
ORING = 32
CRING = 4


def outer(left, right):
    return lax.dot_general(left, right, (((0,), (0,)), ((), ())), preferred_element_type=jnp.float32)


def unpack_kernel(tiles, packed, *refs):
    wide_cols = packed.shape[3]
    many = len(tiles)
    outs, (held, load, store) = refs[:many], refs[2 * many :]
    wide = refs[many : 2 * many]
    copies, base = [], 0
    for w, (nr, nc) in enumerate(tiles):
        copy = pltpu.make_async_copy(packed.at[:, pl.ds(base, nr * nc)], held.at[:, pl.ds(base, nr * nc)], load.at[w])
        copy.start()
        copies.append(copy)
        base += nr * nc
    base, stores = 0, []
    for w, (nr, nc) in enumerate(tiles):
        copies[w].wait()
        for core in range(2):
            for col in range(nc):
                @pl.loop(0, nr)
                def _(row, w=w, core=core, col=col, base=base, nc=nc):
                    wide[w][pl.ds(pl.multiple_of(row * UR, UR), UR), (core * nc + col) * wide_cols : (core * nc + col + 1) * wide_cols] = (
                        held[core, base + row * nc + col].astype(jnp.float32))
        copy = pltpu.make_async_copy(wide[w], outs[w], store.at[w])
        copy.start()
        stores.append(copy)
        base += nr * nc
    for copy in stores:
        copy.wait()


def unpack(packed, count, shapes):
    any_ = pl.BlockSpec(memory_space=pl.ANY)
    out_shape = [jax.ShapeDtypeStruct((r // count, c), jnp.float32) for r, c in shapes]
    tiles = [(r // count // UR, c // 2 // packed.shape[3]) for r, c in shapes]
    dma = pltpu.SemaphoreType.DMA((len(shapes),))
    return pl.pallas_call(
        functools.partial(unpack_kernel, tiles),
        out_shape=out_shape,
        in_specs=[any_],
        out_specs=[any_] * len(shapes),
        scratch_shapes=[pltpu.VMEM(s.shape, s.dtype) for s in out_shape] + [pltpu.VMEM(packed.shape, packed.dtype), dma, dma],
        compiler_params=pltpu.CompilerParams(vmem_limit_bytes=60 * 2**20),
        name="unpack_gradients",
    )(packed)


def dot_nn(left, right):
    return lax.dot_general(left, right, (((1,), (0,)), ((), ())), preferred_element_type=jnp.float32)


def dot_nt(left, right):
    return lax.dot_general(left, right, (((1,), (1,)), ((), ())), preferred_element_type=jnp.float32)


def dot_tn(left, right):
    return lax.dot_general(left, right, (((0,), (0,)), ((), ())), preferred_element_type=jnp.float32)


EPS = 1e-05
COLS = 256


def sigmoid(v):
    return 0.5 * jnp.tanh(0.5 * v) + 0.5


def sum_scratch(count, depth, width):
    dma = pltpu.SemaphoreType.DMA((count + depth - 1,))
    return [pltpu.VMEM((8, width), jnp.float32), pltpu.VMEM((8, width), jnp.float32),
            pltpu.VMEM((count, 8, width), jnp.float32), pltpu.VMEM((depth, 8, width), jnp.float32), dma, dma]


CHUNK = 512
LEAD = 1
BUDGET = 9.0


def forward_kernel(count, depth, heads, shapes, items, saved_names, in_names, out_names, scratch_names, *refs):
    many = len(shapes)
    edges = np.cumsum([0, len(in_names), many, many, len(saved_names), len(out_names), len(scratch_names)])
    groups = [refs[i:j] for i, j in zip(edges[:-1], edges[1:])]
    shards, wholes, saved = groups[1], groups[2], groups[3]
    r = types.SimpleNamespace(**dict(zip(in_names, groups[0])), **dict(zip(out_names, groups[4])), **dict(zip(scratch_names, groups[5])))
    k = types.SimpleNamespace(**{name: i for i, name in enumerate(saved_names)})
    send, recv = r.send, r.recv
    bits = bits_of(count)
    dp, me = lax.axis_index("dp"), lax.axis_index("fsdp")
    core, place = lax.rem(dp, 2), dp // 2
    side = lax.rem(place, 2)
    mate, twin = flip(dp, 1), flip(dp, 2)
    span, width = r.frames.shape
    inner_width = saved[k.inner1].shape[1]
    size = width // heads
    scale = size ** -0.5

    barrier = pltpu.get_barrier_semaphore()
    pl.semaphore_signal(barrier, inc=1, device_id=(mate, me), device_id_type=MESH)
    for mask in range(1, count):
        pl.semaphore_signal(barrier, inc=1, device_id=(dp, flips(me, mask)), device_id_type=MESH)
    for j in range(1, depth):
        pl.semaphore_signal(barrier, inc=1, device_id=(lax.rem(dp + 2 * j, 2 * depth), me), device_id_type=MESH)
    pl.semaphore_wait(barrier, 1 + count - 1 + depth - 1)

    def remote(src, dst, send_sem, recv_sem, device):
        return pltpu.make_async_remote_copy(
            src_ref=src, dst_ref=dst, send_sem=send_sem, recv_sem=recv_sem, device_id=device, device_id_type=MESH)

    wide = r.small.shape[1]
    here = pl.ds(pl.multiple_of(me * wide, 128), wide)
    small_copies = [remote(r.small, r.small_held.at[:, here], r.small_send.at[mask], r.small_recv.at[mask], (dp, flips(me, mask)))
                    for mask in range(1, count)]
    for copy in small_copies:
        copy.start()
    own_copies = [remote(shards[w], wholes[w].at[pl.ds(pl.multiple_of(me * shapes[w][0], 16), shapes[w][0])],
                         r.own_send.at[w], r.own_recv.at[w], (mate, me)) for w in range(many)]
    steps = len(bits)
    kinds = 2 * steps + 3

    def parts(t):
        w, row, rows, col, edge, middle = items[t]
        base = core * (shapes[w][0] // 2) + row
        plane = pl.ds(pl.multiple_of(col + side * edge, 128), edge + middle)
        given = pl.ds(pl.multiple_of(col + side * (edge + middle), 128), edge)
        taken = pl.ds(pl.multiple_of(col + (1 - side) * (edge + middle), 128), edge)
        return w, base, rows, plane, given, taken, edge

    def block(w, owner, start, rows, cols):
        return wholes[w].at[pl.ds(pl.multiple_of(owner * shapes[w][0] + start, 16), rows), cols]

    def plane_send(t, step):
        w, base, rows, plane, *_ = parts(t)
        if step == 0 and (t == 0 or items[t - 1][0] != w):
            own_copies[w].start()
        for piece in range(2):
            order = bits if piece == 0 else bits[::-1]
            start, extent = base + piece * (rows // 2), rows // 2
            for mask in span_of(order[:step]):
                owner = flips(me, mask)
                src = (shards[w].at[pl.ds(pl.multiple_of(start, 16), extent), plane] if mask == 0
                       else block(w, owner, start, extent, plane))
                remote(src, block(w, owner, start, extent, plane), send.at[t, 2 * step + piece],
                       recv.at[t, 2 * step + piece], (dp, flips(me, order[step]))).start()

    def several(t, cols, kind, device):
        w, base, rows, *_ = parts(t)
        for mask in range(1, count):
            ref = block(w, flips(me, mask), base, rows, cols)
            remote(ref, ref, send.at[t, kind], recv.at[t, kind], device).start()

    def sizes(t, kind):
        _, _, rows, _, edge, middle = items[t]
        if kind < 2 * steps:
            return rows // 2 * 2 ** (kind // 2), edge + middle
        return rows * (count - 1), edge if kind != 2 * steps + 1 else edge + middle

    def wait(sems, t, kind):
        rows, cols = sizes(t, kind)
        if cols:
            ref = wholes[items[t][0]].at[pl.ds(0, rows), pl.ds(0, cols)]
            pltpu.make_async_copy(ref, ref, sems.at[t, kind]).wait()

    total = len(items)

    def gather_tick(tick):
        t = tick + LEAD
        if t < total and tick >= 0:
            plane_send(t, 0)
        for step in range(1, steps):
            t = tick - step
            if 0 <= t < total:
                wait(recv, t, 2 * step - 2)
                wait(recv, t, 2 * step - 1)
                plane_send(t, step)
        t = tick - steps
        if 0 <= t < total:
            wait(recv, t, 2 * steps - 2)
            wait(recv, t, 2 * steps - 1)
            _, _, _, plane, given, taken, edge = parts(t)
            if edge:
                several(t, given, 2 * steps, (twin, me))
            several(t, plane, 2 * steps + 1, (mate, me))
        t = tick - steps - 1
        if 0 <= t < total:
            wait(recv, t, 2 * steps)
            if parts(t)[6]:
                several(t, parts(t)[5], 2 * steps + 2, (mate, me))
        t = tick - steps - 2
        if 0 <= t < total:
            wait(recv, t, 2 * steps + 1)
            wait(recv, t, 2 * steps + 2)
            w = items[t][0]
            if t == 0 or items[t - 1][0] != w:
                own_copies[w].wait_recv()
            return t
        return None

    loads = {}

    def load(index, src, dst):
        loads[index] = pltpu.make_async_copy(src, dst, r.load_sem.at[index])
        loads[index].start()

    def ready(*need):
        for index in need:
            loads.pop(index).wait()

    def store(index, src):
        pltpu.make_async_copy(src, saved[index], r.store_sem.at[index]).start()

    stored = set()

    def stored_wait(index):
        pltpu.make_async_copy(saved[index], saved[index], r.store_sem.at[index]).wait()
        stored.add(index)

    gain = lambda n: r.small_all[n : n + 1]
    shift = lambda n: r.small_all[6 + n : 7 + n]

    def normed(v):
        center = v - jnp.mean(v, axis=-1, keepdims=True)
        return center * lax.rsqrt(jnp.mean(center * center, axis=-1, keepdims=True) + EPS)

    def norm_rows(src, n, dst):
        @pl.loop(0, span // 64)
        def _(i):
            rows = pl.ds(pl.multiple_of(i * 64, 64), 64)
            dst[rows] = (normed(src[rows].astype(jnp.float32)) * gain(n) + shift(n)).astype(jnp.bfloat16)

    def begin():
        r.small_held[:, here] = r.small[...]
        for copy in small_copies:
            copy.wait()
        r.small_all[...] = r.small_held[...].astype(jnp.float32)
        r.small_out[...] = r.small_all[...]
        norm_rows(r.frames, 0, r.hid1)
        store(k.hidden1, r.hid1)

    def up_half(hidden, part, parts_of):
        chunks = inner_width // CHUNK // parts_of

        @pl.loop(part * chunks, (part + 1) * chunks)
        def _(i):
            cols = pl.ds(pl.multiple_of(i * CHUNK, CHUNK), CHUNK)
            inner = dot_nn(hidden[...], r.up_vm[:, cols])
            r.inner_vm[:, cols] = inner.astype(jnp.bfloat16)
            r.active_vm[:, cols] = (inner * sigmoid(inner)).astype(jnp.bfloat16)

    def after_early():
        store(k.inner1, r.inner_vm)
        store(k.active1, r.active_vm)
        store(k.x1, r.xa)
        norm_rows(r.xa, 1, r.hid2)
        store(k.hidden2, r.hid2)

    def project(which):
        @pl.loop(0, width // CHUNK)
        def _(i):
            cols = pl.ds(pl.multiple_of(i * CHUNK, CHUNK), CHUNK)
            out = dot_nn(r.hid2[...], r.up_vm[:, pl.ds(pl.multiple_of(i * CHUNK + which * width, CHUNK), CHUNK)])
            if which == 0:
                r.content_vm[:, cols] = (out + r.small_all[12:13, cols]).astype(jnp.bfloat16)
                r.offset_vm[:, cols] = (out + r.small_all[13:14, cols]).astype(jnp.bfloat16)
            else:
                dst = r.keys_vm if which == 1 else r.values_vm
                dst[:, cols] = out.astype(jnp.bfloat16)
        if which == 0:
            store(k.content, r.content_vm)
            store(k.offset, r.offset_vm)
        else:
            store(k.keys, r.keys_vm) if which == 1 else store(k.values, r.values_vm)

    def place_offsets():
        ready(3, 4)

        @pl.loop(0, width // CHUNK)
        def _(i):
            cols = pl.ds(pl.multiple_of(i * CHUNK, CHUNK), CHUNK)
            out = dot_nn(r.table_vm[...], r.up_vm[:, pl.ds(pl.multiple_of(i * CHUNK + 3 * width, CHUNK), CHUNK)])
            r.offsets_vm[:, cols] = out.astype(jnp.bfloat16)
        store(k.offsets, r.offsets_vm)

    def attend(first, last):
        @pl.loop(first, last)
        def _(h):
            cols = pl.ds(pl.multiple_of(h * size, size), size)
            slot = lax.rem(h, 2)
            placed = dot_nt(r.offset_vm[:, cols], r.offsets_vm[:, cols])
            moved = pltpu.roll(placed, span + 1, 1, stride=1, stride_axis=0)[:, :span]
            raw = (dot_nt(r.content_vm[:, cols], r.keys_vm[:, cols]) + moved) * scale
            column = lax.broadcasted_iota(jnp.int32, raw.shape, 1)
            scores = jnp.where(column < r.length[0], raw, -1e30)
            grown = jnp.exp(scores - jnp.max(scores, axis=1, keepdims=True))
            probs = (grown * (1.0 / jnp.sum(grown, axis=1, keepdims=True))).astype(jnp.bfloat16)

            @pl.when(h >= 2)
            def _():
                pltpu.make_async_copy(r.probs_vm.at[slot], saved[k.probs].at[h], r.probs_sem.at[slot]).wait()
            r.probs_vm[slot] = probs
            pltpu.make_async_copy(r.probs_vm.at[slot], saved[k.probs].at[h], r.probs_sem.at[slot]).start()
            r.mixed_vm[:, cols] = dot_nn(probs, r.values_vm[:, cols]).astype(jnp.bfloat16)

    def after_attention():
        for slot in range(2):
            pltpu.make_async_copy(r.probs_vm.at[slot], saved[k.probs].at[0], r.probs_sem.at[slot]).wait()
        store(k.mixed, r.mixed_vm)
        ready(5)

        @pl.loop(0, width // 256)
        def _(i):
            cols = pl.ds(pl.multiple_of(i * 256, 256), 256)
            r.xb[:, cols] = r.xa[:, cols] + dot_nn(r.mixed_vm[...], r.down_vm[0:width, cols])
        store(k.x2, r.xb)
        norm_rows(r.xb, 2, r.hid3)
        store(k.hidden3, r.hid3)

    def valid_mask():
        return jnp.where(lax.broadcasted_iota(jnp.int32, (span, 1), 0) < r.length[0], 1.0, 0.0)

    taps = 5
    half = taps // 2

    def convolve():
        ready(6, 7)
        mask = valid_mask()
        r.padded[0:8] = jnp.zeros((8, 256), jnp.float32)
        r.padded[8 + span : 16 + span] = jnp.zeros((8, 256), jnp.float32)
        r.vec[...] = jnp.zeros_like(r.vec)
        r.vec[2:3] = jnp.full((1, width), 1.0, jnp.float32) * jnp.sum(mask)

        @pl.loop(0, width // 256)
        def _(i):
            cols = pl.ds(pl.multiple_of(i * 256, 256), 256)
            gates = pl.ds(pl.multiple_of(i * 256 + width, 256), 256)
            value = dot_nn(r.hid3[...], r.down_vm[width : 2 * width, cols])
            gate = dot_nn(r.hid3[...], r.down_vm[2 * width : 3 * width, cols])
            r.lifted_vm[:, cols] = value.astype(jnp.bfloat16)
            r.lifted_vm[:, gates] = gate.astype(jnp.bfloat16)
            r.padded[8 : 8 + span] = value * sigmoid(gate) * mask
            out = jnp.zeros((span, 256), jnp.float32)
            for tap in range(taps):
                out = out + r.small_all[14 + tap : 15 + tap, cols] * r.padded[8 + tap - half : 8 + tap - half + span]
            r.conv_vm[:, cols] = out
            masked = out * mask
            r.vec[0:1, cols] = jnp.sum(masked, axis=0, keepdims=True)
            r.vec[1:2, cols] = jnp.sum(masked * out, axis=0, keepdims=True)
        store(k.lifted, r.lifted_vm)
        store(k.convolved, r.conv_vm)

    pair_copy = remote(r.vec, r.pair, r.sum_send.at[0], r.sum_recv.at[0], (mate, me))
    plane_copies = [remote(r.plane.at[me], r.plane.at[me], r.sum_send.at[m], r.sum_recv.at[m], (dp, flips(me, m)))
                    for m in range(1, count)]
    line_copies = [remote(r.line.at[place], r.line.at[place], r.sum_send.at[count - 1 + j], r.sum_recv.at[count - 1 + j],
                          (lax.rem(dp + 2 * j, 2 * depth), me)) for j in range(1, depth)]

    def sum_pair():
        pair_copy.start()

    def sum_plane():
        pair_copy.wait()
        r.plane[me] = r.vec[...] + r.pair[...]
        for copy in plane_copies:
            copy.start()

    def sum_line():
        for copy in plane_copies:
            copy.wait()
        r.line[place] = functools.reduce(jnp.add, [r.plane[f] for f in range(count)])
        for copy in line_copies:
            copy.start()

    def after_conv():
        for copy in line_copies:
            copy.wait()
        sums = functools.reduce(jnp.add, [r.line[z] for z in range(depth)])
        frames = sums[2:3]
        mean = sums[0:1] / frames
        inverse = lax.rsqrt(sums[1:2] / frames - mean * mean + EPS)
        r.stats[...] = jnp.concatenate([mean, inverse, frames, jnp.zeros((5, width), jnp.float32)], axis=0)
        ready(8)

        @pl.loop(0, width // 256)
        def _(i):
            cols = pl.ds(pl.multiple_of(i * 256, 256), 256)
            normal = (r.conv_vm[:, cols] - r.stats[0:1, cols]) * r.stats[1:2, cols]
            scaled = normal * r.small_all[5:6, cols] + r.small_all[11:12, cols]
            r.swished_vm[:, cols] = (scaled * sigmoid(scaled)).astype(jnp.bfloat16)
        store(k.swished, r.swished_vm)
        stored_wait(k.x1)

        @pl.loop(0, width // 256)
        def _(i):
            cols = pl.ds(pl.multiple_of(i * 256, 256), 256)
            r.xa[:, cols] = r.xb[:, cols] + dot_nn(r.swished_vm[...], r.down_vm[3 * width : 4 * width, cols])

    def after_conv_norm():
        store(k.x3, r.xa)
        norm_rows(r.xa, 3, r.hid4)
        store(k.hidden4, r.hid4)
        stored_wait(k.inner1)
        stored_wait(k.active1)

    def late_done():
        store(k.inner4, r.inner_vm)
        store(k.active4, r.active_vm)
        stored_wait(k.x2)

    def final():
        r.edge_grads[...] = jnp.zeros_like(r.edge_grads)

        @pl.loop(0, span // 64)
        def _(i):
            start = pl.multiple_of(i * 64, 64)
            rows = pl.ds(start, 64)
            mask = jnp.where(start + lax.broadcasted_iota(jnp.int32, (64, 1), 0) < r.length[0], 1.0, 0.0)
            v = r.xb[rows]
            center = v - jnp.mean(v, axis=-1, keepdims=True)
            rate = lax.rsqrt(jnp.mean(center * center, axis=-1, keepdims=True) + EPS)
            normal = center * rate
            r.output[rows] = ((normal * gain(4) + shift(4)) * mask).astype(jnp.bfloat16)
            grad = r.cotangent[rows].astype(jnp.float32) * mask
            r.edge_grads[0:1] += jnp.sum(grad * normal, axis=0, keepdims=True)
            r.edge_grads[1:2] += jnp.sum(grad, axis=0, keepdims=True)
            inner = grad * gain(4)
            back = rate * (inner - jnp.mean(inner, axis=-1, keepdims=True)
                           - normal * jnp.mean(inner * normal, axis=-1, keepdims=True))
            r.xa[rows] = back
            r.branch_vm[rows] = (0.5 * back).astype(jnp.bfloat16)
        store(k.grad4, r.xa)
        store(k.branch4, r.branch_vm)

    def down_copies(t, w, sems):
        _, row, rows, *_ = items[t]
        shard, part = shapes[w][0], t - min(u for u in range(total) if items[u][0] == w)
        starts = [f * shard + c * (shard // 2) + row for f in range(count) for c in range(2)]
        return rows, starts, [pltpu.make_async_copy(wholes[w].at[pl.ds(start, rows)], r.down_vm.at[pl.ds(start, rows)], sems.at[part, i])
                              for i, start in enumerate(starts)]

    def down_fetch(t, w, sems):
        for copy in down_copies(t, w, sems)[2]:
            copy.start()

    def down_part(t, w, sems, src, dst):
        rows, starts, copies = down_copies(t, w, sems)
        for copy in copies:
            copy.wait()

        @pl.loop(0, width // 256)
        def _(i):
            cols = pl.ds(pl.multiple_of(i * 256, 256), 256)
            acc = functools.reduce(jnp.add, [dot_nn(r.active_vm[:, s : s + rows], r.down_vm[s : s + rows, cols]) for s in starts])
            dst[:, cols] = src[:, cols].astype(jnp.float32) + 0.5 * acc

    def before_final():
        stored_wait(k.x3)

    up, down = r.up_vm, r.down_vm
    last = [max(t for t in range(total) if items[t][0] == w) for w in range(many)]
    phases = []

    def phase(item, cost, *work):
        phases.append((item, cost, work))

    def fetch(index, src, dst):
        return lambda: load(index, src, dst)

    def call(function, *args):
        return lambda: function(*args)

    phase(-1, 1.5, begin)
    early = [t for t in range(total) if items[t][0] == 0]
    late = [t for t in range(total) if items[t][0] == 7]

    arrivals = []

    def up_loads(ts, w, index, after):
        for n, t in enumerate(ts):
            cols = pl.ds(items[t][3], 2 * items[t][4] + items[t][5])
            arrivals.append((t, after, fetch(index + n, wholes[w].at[:, cols], up.at[:, cols])))

    def down_loads(w, sems, after):
        for t in range(total):
            if items[t][0] == w:
                arrivals.append((t, after, call(down_fetch, t, w, sems)))

    up_loads(early, 0, 0, 0)
    for n, t in enumerate(early):
        phase(t, 3.2, call(ready, n), call(up_half, r.hid1, n, len(early)))
    up_over = len(phases)
    down_loads(1, r.early_sem, 0)
    firsts = [t for t in range(total) if items[t][0] == 1]
    for t in firsts:
        phase(t, 4.5 / len(firsts), call(down_part, t, 1, r.early_sem, r.frames if t == firsts[0] else r.xa, r.xa))
    down_over = len(phases)
    phase(last[1], 1.5, after_early)
    arrivals.append((last[2], up_over, fetch(10, wholes[2], up.at[:, pl.ds(0, 3 * width)])))
    phase(last[2], 2.5, call(ready, 10), call(project, 0), call(project, 1), call(project, 2))
    arrivals.append((last[3], up_over, lambda: (load(3, wholes[3], up.at[:, pl.ds(3 * width, width)]), load(4, r.table, r.table_vm))))
    phase(last[3], 3.0, place_offsets)
    lift_over = len(phases)
    for h in range(0, heads, 2):
        phase(last[3], 2.0, call(attend, h, h + 2))
    arrivals.append((last[4], down_over, fetch(5, wholes[4], down.at[pl.ds(0, width)])))
    phase(last[4], 2.0, after_attention)
    arrivals.append((last[5], down_over, lambda: (load(6, wholes[5].at[:, pl.ds(0, width)], down.at[pl.ds(width, width)]),
                                                  load(7, wholes[5].at[:, pl.ds(width, width)], down.at[pl.ds(2 * width, width)]))))
    phase(last[5], 5.5, convolve)
    phase(last[5], 0.1, sum_pair)
    arrivals.append((last[6], down_over, fetch(8, wholes[6], down.at[pl.ds(3 * width, width)])))
    phase(last[5], 2.0, sum_plane)
    phase(last[5], 3.0, sum_line)
    phase(last[6], 4.0, after_conv)
    conv_over = len(phases)
    phase(last[6], 1.0, after_conv_norm)
    up_loads(late, 7, 11, lift_over)
    for n, t in enumerate(late):
        phase(t, 3.2, call(ready, 11 + n), call(up_half, r.hid4, n, len(late)))
    phase(last[7], 0.1, late_done)
    down_loads(8, r.late_sem, conv_over)
    ends = [t for t in range(total) if items[t][0] == 8]
    for t in ends:
        phase(t, 2.0, call(down_part, t, 8, r.late_sem, r.xa if t == ends[0] else r.xb, r.xb))
    phase(total - 1, 4.0, before_final, final)
    over = 0

    def take_arrivals():
        kept = []
        for t, after, work in arrivals:
            if t <= done and after <= over:
                work()
            else:
                kept.append((t, after, work))
        arrivals[:] = kept

    for t in range(min(LEAD, total)):
        plane_send(t, 0)
    done = -1
    for tick in range(total + steps + 3):
        finished = gather_tick(tick)
        done = max(done, -1 if finished is None else finished)
        take_arrivals()
        budget = BUDGET
        while phases and phases[0][0] <= done and (budget > 0 or done == total - 1):
            _, cost, work = phases.pop(0)
            budget -= cost
            for step in work:
                step()
            over += 1
            take_arrivals()
    for index in range(len(saved) - 1):
        if index not in stored:
            stored_wait(index)
    for w in range(many):
        own_copies[w].wait_send()
    for t in range(total):
        for kind in range(kinds):
            wait(send, t, kind)


def forward(count, depth, heads, frames, cotangent, lengths, shards, small, table, collective_id=1):
    shapes = [s.shape for s in shards]
    items = gather_items(shapes)
    steps, many = len(bits_of(count)), len(shards)
    span, width = frames.shape
    inner = shapes[0][1]
    any_, vmem, smem = (pl.BlockSpec(memory_space=s) for s in (pl.ANY, pltpu.VMEM, pltpu.SMEM))
    bf, fl = jnp.bfloat16, jnp.float32
    S, dma = jax.ShapeDtypeStruct, pltpu.SemaphoreType.DMA
    V = lambda shape, dtype=bf: pltpu.VMEM(shape, dtype)
    ins = dict(length=(lengths, smem), frames=(frames, vmem), cotangent=(cotangent, vmem), table=(table, any_), small=(small, vmem))
    flat, flat32, tall = S((span, width), bf), S((span, width), fl), S((span, inner), bf)
    saved = dict(hidden1=flat, inner1=tall, active1=tall, x1=flat32, hidden2=flat, content=flat, offset=flat, keys=flat, values=flat,
                 offsets=S(table.shape, bf), mixed=flat, x2=flat32, hidden3=flat, lifted=S((span, 2 * width), bf), convolved=flat32,
                 swished=flat, x3=flat32, hidden4=flat, inner4=tall, active4=tall, grad4=flat32, branch4=flat,
                 probs=S((heads, span, span), bf))
    outs = dict(small_out=S((small.shape[0], width), fl), stats=S((8, width), fl), edge_grads=S((8, width), fl), output=flat)
    vec, pair, plane, line, sum_send, sum_recv = sum_scratch(count, depth, width)
    flat_vm, flat32_vm, gather_sems = V((span, width)), V((span, width), fl), dma((len(items), 2 * steps + 3))
    scratch = dict(
        send=gather_sems, recv=gather_sems, own_send=dma((many,)), own_recv=dma((many,)),
        small_send=dma((count,)), small_recv=dma((count,)), load_sem=dma((16,)), store_sem=dma((len(saved),)), probs_sem=dma((2,)),
        early_sem=dma((8, 2 * count)), late_sem=dma((8, 2 * count)),
        small_held=V((small.shape[0], width)), small_all=V((small.shape[0], width), fl),
        up_vm=V((width, inner)), down_vm=V((inner, width)), xa=flat32_vm, xb=flat32_vm,
        hid1=flat_vm, hid2=flat_vm, hid3=flat_vm, hid4=flat_vm, inner_vm=V((span, inner)), active_vm=V((span, inner)),
        content_vm=flat_vm, offset_vm=flat_vm, keys_vm=flat_vm, values_vm=flat_vm, table_vm=V(table.shape), offsets_vm=V(table.shape),
        probs_vm=V((2, span, span)), mixed_vm=flat_vm, lifted_vm=V((span, 2 * width)), conv_vm=flat32_vm, swished_vm=flat_vm,
        branch_vm=flat_vm, padded=V((span + 16, 256), fl),
        vec=vec, pair=pair, plane=plane, line=line, sum_send=sum_send, sum_recv=sum_recv)
    whole = [S((rows * count, cols), bf) for rows, cols in shapes]
    values = pl.pallas_call(
        functools.partial(forward_kernel, count, depth, heads, shapes, items, list(saved), list(ins), list(outs), list(scratch)),
        out_shape=whole + list(saved.values()) + list(outs.values()),
        in_specs=[b for _, b in ins.values()] + [any_] * many,
        out_specs=[any_] * (many + len(saved)) + [vmem] * len(outs),
        scratch_shapes=list(scratch.values()),
        compiler_params=pltpu.CompilerParams(collective_id=collective_id, has_side_effects=True, vmem_limit_bytes=63 * 2**20),
        name="forward",
    )(*[v for v, _ in ins.values()], *shards)
    return values[:many], types.SimpleNamespace(**dict(zip(list(saved) + list(outs), values[many:])))


COLS = 256
SLICE = 512


def backward_kernel(count, depth, heads, shapes, in_names, out_names, scratch_names, *refs):
    edges = np.cumsum([0, len(in_names), len(out_names), len(scratch_names)])
    groups = [refs[i:j] for i, j in zip(edges[:-1], edges[1:])]
    r = types.SimpleNamespace(**dict(zip(in_names, groups[0])), **dict(zip(out_names, groups[1])), **dict(zip(scratch_names, groups[2])))
    many, unit = len(shapes), unit_cols(count)
    lefts = [r.active4, r.hidden4, r.swished, r.hidden3, r.mixed, r.table, r.hidden2, r.active1, r.hidden1]
    rights = [r.branch4, r.inner_grad4, r.out_grad3, r.lifted_grad, r.out_grad2, r.offsets_grad, r.joint_grad, r.branch1, r.inner_grad1]
    bits = bits_of(count)
    steps, half = len(bits), depth // 2
    dp, me = lax.axis_index("dp"), lax.axis_index("fsdp")
    core, place = lax.rem(dp, 2), dp // 2
    mate = flip(dp, 1)
    low = place < half
    level = jnp.minimum(place, depth - 1 - place)
    inward = jnp.where(low, dp + 2, dp - 2)
    outward = jnp.where(low, dp - 2, dp + 2)
    span, width = r.grad4.shape
    inner_width = r.inner4.shape[1]
    size = width // heads
    scale = size ** -0.5

    def remote(src, dst, send, recv, device):
        return pltpu.make_async_remote_copy(
            src_ref=src, dst_ref=dst, send_sem=send, recv_sem=recv, device_id=device, device_id_type=MESH)

    def loading(src, dst, index):
        return pltpu.make_async_copy(src, dst, r.load_sem.at[index])

    def storing(src, dst, index):
        return pltpu.make_async_copy(src, dst, r.store_sem.at[index])

    units = [(rows // count // UR) * (cols // 2 // unit) for rows, cols, _ in shapes]
    bases = [int(b) for b in np.cumsum([0] + units)]
    whole = bases[-1]

    def unit_copies(w, i, slot):
        rows, cols, deep = shapes[w]
        rows, chunks = rows // count, cols // 2 // unit
        row, col = i // chunks, lax.rem(i, chunks)
        copies = []
        for m in range(count):
            src = lefts[w].at[:, pl.ds(pl.multiple_of(flips(me, m) * rows + row * UR, UR), UR)]
            copies.append(pltpu.make_async_copy(src, r.a_st.at[slot, pl.ds(0, deep), pl.ds(m * UR, UR)], r.st_sem.at[slot, m]))
        for n, owner in enumerate((1 - core, core)):
            src = rights[w].at[:, pl.ds(pl.multiple_of(owner * (cols // 2) + col * unit, unit), unit)]
            copies.append(pltpu.make_async_copy(src, r.b_st.at[slot, n, pl.ds(0, deep)], r.st_sem.at[slot, count + n]))
        return copies

    def fetch_unit(u):
        for w in range(many):
            @pl.when(jnp.logical_and(u >= bases[w], u < bases[w + 1]))
            def _(w=w):
                for copy in unit_copies(w, u - bases[w], lax.rem(u, 2)):
                    copy.start()

    def c_copy(u):
        s = lax.rem(u, CRING)
        return remote(r.snd_c.at[s], r.rcv_c.at[s], r.c_send.at[s], r.c_recv.at[s], (mate, me))

    def d_copy(j, piece, u):
        s = lax.rem(u, RING)
        order = bits if piece == 0 else bits[::-1]
        return remote(d_snd[j].at[s, piece], d_rcv[j].at[s, piece],
                      r.d_send.at[j, piece, s], r.d_recv.at[j, piece, s], (dp, flip(me, order[j])))

    d_snd = [r.d_snd0, r.d_snd1, r.d_snd2][:steps]
    d_rcv = [r.d_rcv0, r.d_rcv1, r.d_rcv2][:steps]

    def zi_copy(u):
        s = lax.rem(u, ZRING)
        return remote(r.z_snd.at[s], r.z_acc.at[s], r.zi_send.at[s], r.za_recv.at[s], (inward, me))

    def zm_copy(u):
        s = lax.rem(u, ZRING)
        return remote(r.z_snd.at[s], r.z_mid.at[s], r.zi_send.at[s], r.zm_recv.at[s], (inward, me))

    def loc_copy(u):
        s = lax.rem(u, ZRING)
        return pltpu.make_async_copy(r.total.at[s], r.packed.at[core, u], r.loc_sem.at[s])

    def mt_copy(u, src):
        s = lax.rem(u, ORING)
        return remote(src, r.packed.at[core, u], r.mt_send.at[s], r.mt_recv.at[s], (mate, me))

    def zo_copy(u, src):
        s = lax.rem(u, ORING)
        return remote(src, r.packed.at[core, u], r.zo_send.at[s], r.zo_recv.at[s], (outward, me))

    def first(u):
        slot, s = lax.rem(u, 2), lax.rem(u, CRING)
        depths = sorted(set(deep for *_, deep in shapes))
        for deep in depths:
            ws = [w for w in range(many) if shapes[w][2] == deep]
            cond = functools.reduce(jnp.logical_or, [jnp.logical_and(u >= bases[w], u < bases[w + 1]) for w in ws])

            @pl.when(cond)
            def _(deep=deep, w=ws[0]):
                for copy in unit_copies(w, 0, slot):
                    copy.wait()
                left = r.a_st[slot, 0:deep]
                r.snd_c[s] = outer(left, r.b_st[slot, 0, 0:deep]).astype(jnp.bfloat16).reshape(count, UR, unit)
                c_copy(u).start()
                r.own[lax.rem(u, RING)] = outer(left, r.b_st[slot, 1, 0:deep]).reshape(count, UR, unit)

    def rows_of(piece):
        return slice(piece * (UR // 2), (piece + 1) * (UR // 2))

    def second(u):
        c_copy(u).wait()
        s, c = lax.rem(u, RING), lax.rem(u, CRING)
        for piece in range(2):
            order = bits if piece == 0 else bits[::-1]
            rs = rows_of(piece)
            for k, m in enumerate(span_of(order[1:])):
                x = m + order[0]
                d_snd[0][s, piece, k] = (r.own[s, x, rs] + r.rcv_c[c, x, rs].astype(jnp.float32)).astype(jnp.bfloat16)
            d_copy(0, piece, u).start()
        for piece in range(2):
            order = bits if piece == 0 else bits[::-1]
            rs = rows_of(piece)
            for m in span_of(order[1:]):
                r.own[s, m, rs] = r.own[s, m, rs] + r.rcv_c[c, m, rs].astype(jnp.float32)

    def onward(j, u):
        s = lax.rem(u, RING)
        for piece in range(2):
            d_copy(j - 1, piece, u).wait()
            order = bits if piece == 0 else bits[::-1]
            rs = rows_of(piece)
            spans, keep = span_of(order[j:]), span_of(order[j + 1 :])
            for k, m in enumerate(spans):
                if m not in keep:
                    d_snd[j][s, piece, keep.index(m - order[j])] = (
                        r.own[s, m, rs] + d_rcv[j - 1][s, piece, k].astype(jnp.float32)).astype(jnp.bfloat16)
            d_copy(j, piece, u).start()
            for k, m in enumerate(spans):
                if m in keep:
                    r.own[s, m, rs] = r.own[s, m, rs] + d_rcv[j - 1][s, piece, k].astype(jnp.float32)

    def plane_done(u):
        s, z = lax.rem(u, RING), lax.rem(u, ZRING)
        for piece in range(2):
            d_copy(steps - 1, piece, u).wait()
            rs = rows_of(piece)
            r.zsum[z, rs] = r.own[s, 0, rs] + d_rcv[steps - 1][s, piece, 0].astype(jnp.float32)

        @pl.when(level == 0)
        def _():
            r.z_snd[z] = r.zsum[z].astype(jnp.bfloat16)
            if half == 1:
                zm_copy(u).start()
            else:
                zi_copy(u).start()

    def climb(j, u):
        z = lax.rem(u, ZRING)

        @pl.when(level == j - 1)
        def _():
            zi_copy(u).wait_send()

        @pl.when(level == j)
        def _():
            zi_copy(u).wait_recv()
            r.z_snd[z] = (r.zsum[z] + r.z_acc[z].astype(jnp.float32)).astype(jnp.bfloat16)
            if j == half - 1:
                zm_copy(u).start()
            else:
                zi_copy(u).start()

    def middle(u):
        z = lax.rem(u, ZRING)

        @pl.when(level == half - 1)
        def _():
            zm_copy(u).wait()
            r.total[z] = (r.z_snd[z].astype(jnp.float32) + r.z_mid[z].astype(jnp.float32)).astype(jnp.bfloat16)
            if half > 1:
                zo_copy(u, r.total.at[z]).start()
            mt_copy(u, r.total.at[z]).start()
            loc_copy(u).start()

    def descend(j, u):
        z = lax.rem(u, ZRING)

        @pl.when(level == half - j)
        def _():
            src = r.total.at[z] if j == 1 else r.packed.at[core, u]
            zo_copy(u, src).wait_send()

        @pl.when(level == half - 1 - j)
        def _():
            zo_copy(u, r.packed.at[core, u]).wait_recv()
            if j < half - 1:
                zo_copy(u, r.packed.at[core, u]).start()
            mt_copy(u, r.packed.at[core, u]).start()

    def finish(u):
        z = lax.rem(u, ZRING)

        @pl.when(level == half - 1)
        def _():
            loc_copy(u).wait()
        mt_copy(u, r.total.at[z]).wait()

    stages = [(1, second)]
    at = 1
    for j in range(1, steps):
        at += LAG
        stages.append((at, functools.partial(onward, j)))
    at += LAG
    stages.append((at, plane_done))
    for j in range(1, half):
        at += LAG
        stages.append((at, functools.partial(climb, j)))
    at += LAG
    stages.append((at, middle))
    for j in range(1, half):
        at += LAG
        stages.append((at, functools.partial(descend, j)))
    at += LAG
    stages.append((at, finish))

    slices = inner_width // SLICE

    def slice_streams(i, up, inner):
        slot, cols = lax.rem(i, 2), pl.ds(pl.multiple_of(i * SLICE, SLICE), SLICE)
        return (pltpu.make_async_copy(up.at[:, cols], r.up_st.at[slot], r.up_sem.at[slot]),
                pltpu.make_async_copy(inner.at[:, cols], r.in_st.at[slot], r.in_sem.at[slot]))

    def slice_store(i, dst):
        slot, cols = lax.rem(i, 2), pl.ds(pl.multiple_of(i * SLICE, SLICE), SLICE)
        return pltpu.make_async_copy(r.ig_st.at[slot], dst.at[:, cols], r.ig_sem.at[slot])

    def slices_begin(down, up, inner):
        for i in range(slices):
            rows = pl.ds(i * SLICE, SLICE)
            pltpu.make_async_copy(down.at[rows], r.w_vm.at[rows], r.w_sem.at[i]).start()
        for i in range(2):
            for copy in slice_streams(i, up, inner):
                copy.start()

    def slice_work(i, late):
        slot = lax.rem(i, 2)
        rows = pl.ds(pl.multiple_of(i * SLICE, SLICE), SLICE)
        pltpu.make_async_copy(r.late_down.at[rows], r.w_vm.at[rows], r.w_sem.at[i]).wait()
        for copy in slice_streams(i, r.late_up, r.inner4):
            copy.wait()

        @pl.when(i >= 2)
        def _():
            slice_store(i, r.inner_grad4).wait()

        @pl.loop(0, SLICE // COLS)
        def _(c):
            part = pl.ds(pl.multiple_of(c * COLS, COLS), COLS)
            active_grad = dot_nt(r.og[...], r.w_vm[pl.ds(pl.multiple_of(i * SLICE + c * COLS, COLS), COLS)])
            inner = r.in_st[slot, :, part].astype(jnp.float32)
            gate = sigmoid(inner)
            r.ig_st[slot, :, part] = (active_grad * (gate * (1.0 + inner * (1.0 - gate)))).astype(jnp.bfloat16)

        @pl.when(late)
        def _():
            slice_store(i, r.inner_grad4).start()

        @pl.when(jnp.logical_not(late))
        def _():
            slice_store(i, r.inner_grad1).start()

        @pl.loop(0, width // COLS)
        def _(c):
            part = pl.ds(pl.multiple_of(c * COLS, COLS), COLS)
            r.acc[:, part] += dot_nt(r.ig_st[slot], r.up_st[slot, part])

        @pl.when(jnp.logical_and(late, i < slices - 2))
        def _():
            for copy in slice_streams(i + 2, r.late_up, r.inner4):
                copy.start()

        @pl.when(jnp.logical_and(jnp.logical_not(late), i < slices - 2))
        def _():
            for copy in slice_streams(i + 2, r.early_up, r.inner1):
                copy.start()

    def slices_over(dst):
        for i in range(2):
            slice_store(i, dst).wait()

    def norm_back(n, factor):
        gain = r.small_all[pl.ds(n, 1)]
        r.sums[...] = jnp.zeros_like(r.sums)

        @pl.loop(0, span // 64)
        def _(i):
            rows = pl.ds(pl.multiple_of(i * 64, 64), 64)
            v, grad = r.x[rows], r.acc[rows]
            center = v - jnp.mean(v, axis=-1, keepdims=True)
            rate = lax.rsqrt(jnp.mean(center * center, axis=-1, keepdims=True) + EPS)
            normal = center * rate
            r.sums[0:1] += jnp.sum(grad * normal, axis=0, keepdims=True)
            r.sums[1:2] += jnp.sum(grad, axis=0, keepdims=True)
            inner = grad * gain
            back = r.grad[rows] + rate * (inner - jnp.mean(inner, axis=-1, keepdims=True)
                                          - normal * jnp.mean(inner * normal, axis=-1, keepdims=True))
            r.grad[rows] = back
            r.og[rows] = (factor * back).astype(jnp.bfloat16)
        r.small_buf[pl.ds(n, 1)] = r.sums[0:1]
        r.small_buf[pl.ds(n + 6, 1)] = r.sums[1:2]

    def valid_mask():
        return jnp.where(lax.broadcasted_iota(jnp.int32, (span, 1), 0) < r.length[0], 1.0, 0.0)

    taps = 5
    reach = taps // 2

    def conv_first(j):
        cols = pl.ds(pl.multiple_of(j * COLS, COLS), COLS)
        mask = valid_mask()
        swish_grad = dot_nt(r.og[...], r.w_vm[cols])
        normal = (r.x[:, cols] - r.stats[0:1, cols]) * r.stats[1:2, cols]
        scaled = normal * r.small_all[5:6, cols] + r.small_all[11:12, cols]
        gate = sigmoid(scaled)
        scaled_grad = swish_grad * (gate * (1.0 + scaled * (1.0 - gate)))
        r.acc[:, cols] = scaled_grad
        masked = scaled_grad * mask
        r.vec[0:1, cols] = jnp.sum(masked, axis=0, keepdims=True)
        r.vec[1:2, cols] = jnp.sum(masked * normal, axis=0, keepdims=True)

    def conv_second(j):
        cols = pl.ds(pl.multiple_of(j * COLS, COLS), COLS)
        gates = pl.ds(pl.multiple_of(j * COLS + width, COLS), COLS)
        mask = valid_mask()
        normal = (r.x[:, cols] - r.stats[0:1, cols]) * r.stats[1:2, cols]
        inner = mask * ((r.vec[0:1, cols] + normal * r.vec[1:2, cols]) / r.stats[2:3, cols])
        conv_grad = r.stats[1:2, cols] * r.small_all[5:6, cols] * (r.acc[:, cols] - inner)
        r.padded[8 : 8 + span] = conv_grad
        up, gate = r.lifted_vm[:, cols].astype(jnp.float32), sigmoid(r.lifted_vm[:, gates].astype(jnp.float32))
        r.gated[8 : 8 + span] = up * gate * mask
        total = jnp.zeros((span, COLS), jnp.float32)
        for tap in range(taps):
            total = total + r.small_all[14 + tap : 15 + tap, cols] * r.padded[8 - tap + reach : 8 - tap + reach + span]
            moved = r.gated[8 + tap - reach : 8 + tap - reach + span]
            r.small_buf[14 + tap : 15 + tap, cols] = jnp.sum(moved * conv_grad, axis=0, keepdims=True)
        total = total * mask
        r.lg_vm[:, cols] = (total * gate).astype(jnp.bfloat16)
        r.lg_vm[:, gates] = (total * up * gate * (1.0 - gate)).astype(jnp.bfloat16)

    pair_copy = remote(r.vec, r.pair, r.sum_send.at[0], r.sum_recv.at[0], (mate, me))
    plane_copies = [remote(r.plane.at[me], r.plane.at[me], r.sum_send.at[m], r.sum_recv.at[m], (dp, flips(me, m)))
                    for m in range(1, count)]
    line_to = [(lax.rem(dp + 2 * j, 2 * depth), me) for j in range(1, depth)]
    line_copies = [remote(r.line.at[place], r.line.at[place], r.sum_send.at[count + j], r.sum_recv.at[count + j], line_to[j])
                   for j in range(depth - 1)]

    def sum_plane():
        pair_copy.wait()
        r.plane[me] = r.vec[...] + r.pair[...]
        for copy in plane_copies:
            copy.start()

    def sum_line():
        for copy in plane_copies:
            copy.wait()
        r.line[place] = functools.reduce(jnp.add, [r.plane[f] for f in range(count)])
        for copy in line_copies:
            copy.start()

    def sum_over():
        for copy in line_copies:
            copy.wait()
        r.vec[...] = functools.reduce(jnp.add, [r.line[z] for z in range(depth)])

    def head_copies(h):
        slot, cols = lax.rem(h, 2), pl.ds(pl.multiple_of(h * size, size), size)
        copies = [pltpu.make_async_copy(src.at[:, cols], r.head_st.at[slot, n], r.head_sem.at[slot, n])
                  for n, src in enumerate((r.content, r.offset, r.keys, r.values))]
        copies.append(pltpu.make_async_copy(r.offsets.at[:, cols], r.place_st.at[slot], r.head_sem.at[slot, 4]))
        copies.append(pltpu.make_async_copy(r.probs.at[h], r.probs_st.at[slot], r.head_sem.at[slot, 5]))
        return copies

    def offsets_store(h):
        slot, cols = lax.rem(h, 2), pl.ds(pl.multiple_of(h * size, size), size)
        return pltpu.make_async_copy(r.turned_st.at[slot], r.offsets_grad.at[:, cols], r.turned_sem.at[slot])

    def attend_back(h):
        slot, cols = lax.rem(h, 2), pl.ds(pl.multiple_of(h * size, size), size)
        for copy in head_copies(h):
            copy.wait()

        @pl.when(h >= 2)
        def _():
            offsets_store(h).wait()
        content, offset, key, value = (r.head_st[slot, n] for n in range(4))
        mixed_grad, p = r.mg_vm[:, cols], r.probs_st[slot]
        key_cols = pl.ds(pl.multiple_of(h * size + width, size), size)
        value_cols = pl.ds(pl.multiple_of(h * size + 2 * width, size), size)
        prob_grad = dot_nt(mixed_grad, value)
        r.joint_vm[:, value_cols] = dot_tn(p, mixed_grad).astype(jnp.bfloat16)
        weights = p.astype(jnp.float32)
        product = weights * prob_grad
        score_grad = product - weights * jnp.sum(product, axis=1, keepdims=True)
        raw_grad = (score_grad * scale).astype(jnp.bfloat16)
        content_grad = dot_nn(raw_grad, key)
        r.joint_vm[:, key_cols] = dot_tn(raw_grad, content).astype(jnp.bfloat16)
        turn = r.turn[...]
        turned = dot_nn(turn, raw_grad)
        wide = jnp.concatenate([turned, jnp.zeros_like(turned)], axis=1)
        placed = pltpu.roll(wide, 0, 1, stride=1, stride_axis=0).astype(jnp.bfloat16)
        turned_offset = dot_nn(turn, offset).astype(jnp.bfloat16)
        r.turned_st[slot] = dot_tn(placed, turned_offset).astype(jnp.bfloat16)
        offsets_store(h).start()
        turned_grad = dot_nn(placed, r.place_st[slot])
        high = turned_grad.astype(jnp.bfloat16)
        small = (turned_grad - high.astype(jnp.float32)).astype(jnp.bfloat16)
        offset_grad = dot_nn(turn, high) + dot_nn(turn, small)
        r.joint_vm[:, cols] = (content_grad + offset_grad).astype(jnp.bfloat16)
        r.small_buf[12:13, cols] = jnp.sum(content_grad, axis=0, keepdims=True)
        r.small_buf[13:14, cols] = jnp.sum(turned_grad, axis=0, keepdims=True)

        @pl.when(h < heads - 2)
        def _():
            for copy in head_copies(h + 2):
                copy.start()

    narrow = r.small_out.shape[1]

    def columns(f):
        return pl.ds(pl.multiple_of(f * narrow, 128), narrow)

    small_pair = remote(r.small_buf, r.s_pair, r.s_send.at[0], r.s_recv.at[0], (mate, me))
    small_plane = [remote(r.s_both.at[:, columns(flips(me, m))], r.s_plane.at[me], r.s_send.at[m], r.s_recv.at[m], (dp, flips(me, m)))
                   for m in range(1, count)]
    small_line = [remote(r.s_line.at[place], r.s_line.at[place], r.s_send.at[count + j], r.s_recv.at[count + j], line_to[j])
                  for j in range(depth - 1)]

    def small_second():
        small_pair.wait()
        r.s_both[...] = r.small_buf[...] + r.s_pair[...]
        for copy in small_plane:
            copy.start()
        r.s_plane[me] = r.s_both[:, columns(me)]

    def small_third():
        for copy in small_plane:
            copy.wait()
        r.s_line[place] = functools.reduce(jnp.add, [r.s_plane[f] for f in range(count)])
        for copy in small_line:
            copy.start()

    def small_last():
        for copy in small_line:
            copy.wait()
        r.small_out[...] = functools.reduce(jnp.add, [r.s_line[z] for z in range(depth)])

    def block(n):
        return r.w_vm.at[pl.ds(n * width, width)]

    conv_loads = [loading(r.convolved, r.x, 2), loading(r.lifted, r.lifted_vm, 3), loading(r.pointwise_down, block(0), 4),
                  loading(r.pointwise_up.at[:, pl.ds(0, width)], block(1), 5),
                  loading(r.pointwise_up.at[:, pl.ds(width, width)], block(2), 6), loading(r.heads_out, block(3), 7)]
    query_loads = [loading(r.heads_in.at[:, pl.ds(n * width, width)], block(n), 9 + n) for n in range(3)]
    state_load, older_load = loading(r.x2, r.x, 8), loading(r.x1, r.x, 12)
    grad3_store, lifted_store = storing(r.og, r.out_grad3, 0), storing(r.lg_vm, r.lifted_grad, 1)
    grad2_store, joint_store = storing(r.og, r.out_grad2, 2), storing(r.joint_vm, r.joint_grad, 3)
    branch_store, frames_store = storing(r.og, r.branch1, 4), storing(r.grad, r.frames_grad, 5)

    def hidden_cols(first_col, last_col, parts):
        @pl.loop(first_col, last_col)
        def _(c):
            cols = pl.ds(pl.multiple_of(c * COLS, COLS), COLS)
            r.acc[:, cols] = functools.reduce(jnp.add, [
                dot_nt(src[:, a * width : (a + 1) * width], r.w_vm[pl.ds(pl.multiple_of(b * width + c * COLS, COLS), COLS)])
                for src, a, b in parts])

    def chain(tick):
        def when(*ticks):
            cond = functools.reduce(jnp.logical_or, [tick == t for t in ticks])
            return pl.when(cond)

        late = tick < 4

        @pl.when(jnp.logical_or(late, jnp.logical_and(tick >= 24, tick < 28)))
        def _():
            begin = 2 * jnp.where(late, tick, tick - 24)

            @pl.loop(0, 2)
            def _(k):
                slice_work(begin + k, late)

        @when(4)
        def _():
            slices_over(r.inner_grad4)
            for copy in conv_loads[2:]:
                copy.start()

        @when(31)
        def _():
            r.x[...] = r.frames[...].astype(jnp.float32)
            slices_over(r.inner_grad1)

        @when(4, 12, 23, 32)
        def _():
            n = jnp.where(tick == 4, 3, jnp.where(tick == 12, 2, jnp.where(tick == 23, 1, 0)))
            norm_back(n, jnp.where(tick == 23, 0.5, 1.0))

        @when(4)
        def _():
            grad3_store.start()
            conv_loads[0].start()
            conv_loads[1].start()

        @when(5)
        def _():
            for copy in conv_loads[:3]:
                copy.wait()

        @when(5, 6)
        def _():
            @pl.loop(0, 2)
            def _(k):
                conv_first(2 * (tick - 5) + k)

        @when(6)
        def _():
            r.small_buf[5:6] = r.vec[1:2]
            r.small_buf[11:12] = r.vec[0:1]
            pair_copy.start()

        when(7)(sum_plane)
        when(8)(sum_line)

        @when(9)
        def _():
            sum_over()

        @when(9, 10)
        def _():
            @pl.loop(0, 2)
            def _(k):
                conv_second(2 * (tick - 9) + k)

        @when(10)
        def _():
            lifted_store.start()
            state_load.start()
            grad3_store.wait()

        @when(11)
        def _():
            conv_loads[3].wait()
            conv_loads[4].wait()
            hidden_cols(0, width // COLS, [(r.lg_vm, 0, 1), (r.lg_vm, 1, 2)])
            state_load.wait()
            for h in range(2):
                for copy in head_copies(h):
                    copy.start()

        @when(12)
        def _():
            lifted_store.wait()
            grad2_store.start()
            older_load.start()
            conv_loads[5].wait()

            @pl.loop(0, width // COLS)
            def _(c):
                cols = pl.ds(pl.multiple_of(c * COLS, COLS), COLS)
                r.mg_vm[:, cols] = dot_nt(r.og[...], r.w_vm[pl.ds(pl.multiple_of(3 * width + c * COLS, COLS), COLS)]).astype(jnp.bfloat16)

        @when(13)
        def _():
            for copy in query_loads:
                copy.start()

        @pl.when(jnp.logical_and(tick >= 13, tick < 13 + heads))
        def _():
            attend_back(tick - 13)

        @when(13 + heads - 1)
        def _():
            joint_store.start()

        when(19)(grad2_store.wait)
        when(29)(branch_store.wait)
        joint_parts = [(r.joint_vm, n, n) for n in range(3)]

        @when(21)
        def _():
            for h in range(2):
                offsets_store(h).wait()
            for copy in query_loads:
                copy.wait()
            older_load.wait()

        @when(21, 22)
        def _():
            begin = (width // COLS // 2) * (tick - 21)
            hidden_cols(begin, begin + width // COLS // 2, joint_parts)

        @when(23)
        def _():
            joint_store.wait()
            branch_store.start()
            r.acc[...] = jnp.zeros_like(r.acc)
            slices_begin(r.early_down, r.early_up, r.inner1)

        @when(32)
        def _():
            frames_store.start()
            small_pair.start()

        when(34)(small_second)
        when(36)(small_third)

        @when(38)
        def _():
            small_last()
            frames_store.wait()

    barrier = pltpu.get_barrier_semaphore()
    pl.semaphore_signal(barrier, inc=1, device_id=(mate, me), device_id_type=MESH)
    for mask in range(1, count):
        pl.semaphore_signal(barrier, inc=1, device_id=(dp, flips(me, mask)), device_id_type=MESH)
    for device in line_to:
        pl.semaphore_signal(barrier, inc=1, device_id=device, device_id_type=MESH)
    starts = [loading(r.grad4, r.grad, 0), loading(r.x3, r.x, 1), loading(r.branch4, r.og, 13)]
    for copy in starts:
        copy.start()
    fetch_unit(jnp.int32(0))
    slices_begin(r.late_down, r.late_up, r.inner4)
    r.acc[...] = jnp.zeros_like(r.acc)
    r.small_buf[...] = jnp.zeros_like(r.small_buf)
    r.small_buf[4:5] = r.edge_grads[0:1]
    r.small_buf[10:11] = r.edge_grads[1:2]
    r.vec[...] = jnp.zeros_like(r.vec)
    for ref in (r.padded, r.gated):
        ref[0:8] = jnp.zeros((8, COLS), jnp.float32)
        ref[8 + span : 16 + span] = jnp.zeros((8, COLS), jnp.float32)
    row = lax.broadcasted_iota(jnp.int32, (span, span), 0)
    column = lax.broadcasted_iota(jnp.int32, (span, span), 1)
    r.turn[...] = jnp.where(row + column == span - 1, 1.0, 0.0).astype(jnp.bfloat16)
    pl.semaphore_wait(barrier, 1 + count - 1 + depth - 1)
    for copy in starts:
        copy.wait()

    @pl.loop(0, whole + at + 1)
    def _(tick):
        @pl.when(tick + 1 < whole)
        def _():
            fetch_unit(tick + 1)

        @pl.when(tick < whole)
        def _():
            first(tick)
        for lag, stage in stages:
            pl.when(jnp.logical_and(tick >= lag, tick - lag < whole))(functools.partial(stage, tick - lag))
        chain(tick)


def backward(count, depth, heads, frames, lengths, wholes, f, table, collective_id=2):
    early_up, early_down, heads_in, _, heads_out, pointwise_up, pointwise_down, late_up, late_down = wholes
    any_, vmem, smem = (pl.BlockSpec(memory_space=s) for s in (pl.ANY, pltpu.VMEM, pltpu.SMEM))
    bf, fl = jnp.bfloat16, jnp.float32
    S, dma = jax.ShapeDtypeStruct, pltpu.SemaphoreType.DMA
    V = lambda shape, dtype=bf: pltpu.VMEM(shape, dtype)
    span, width = frames.shape
    inner = early_up.shape[1]
    size, unit = width // heads, unit_cols(count)
    far = dict(
        table=table, early_up=early_up, early_down=early_down, heads_in=heads_in, heads_out=heads_out, pointwise_up=pointwise_up,
        pointwise_down=pointwise_down, late_up=late_up, late_down=late_down, active4=f.active4, branch4=f.branch4, inner4=f.inner4,
        hidden4=f.hidden4, grad4=f.grad4, x3=f.x3, convolved=f.convolved, lifted=f.lifted, swished=f.swished, hidden3=f.hidden3,
        x2=f.x2, mixed=f.mixed, content=f.content, offset=f.offset, keys=f.keys, values=f.values, probs=f.probs, offsets=f.offsets,
        hidden2=f.hidden2, x1=f.x1, active1=f.active1, inner1=f.inner1, hidden1=f.hidden1)
    near = dict(frames=frames, small_all=f.small_out, stats=f.stats, edge_grads=f.edge_grads)
    shapes = [(inner, width, span), (width, inner, span), (width, width, span), (width, 2 * width, span), (width, width, span),
              (width, width, table.shape[0]), (width, 3 * width, span), (inner, width, span), (width, inner, span)]
    units = sum((rows // count // UR) * (cols // 2 // unit) for rows, cols, _ in shapes)
    rows = f.small_out.shape[0]
    flat, tall = S((span, width), bf), S((span, inner), bf)
    far_outs = dict(packed=S((2, units, UR, unit), bf), frames_grad=S((span, width), fl), inner_grad4=tall, out_grad3=flat,
                    lifted_grad=S((span, 2 * width), bf), out_grad2=flat, offsets_grad=S(table.shape, bf),
                    joint_grad=S((span, 3 * width), bf), branch1=flat, inner_grad1=tall)
    near_outs = dict(small_out=S((rows, width // count), fl))
    vec, pair, plane, line, _, _ = sum_scratch(count, depth, width)
    bits = bits_of(count)
    deepest = max(deep for *_, deep in shapes)
    block_ring = V((CRING, count, UR, unit))
    z_ring = V((ZRING, UR, unit))
    scratch = dict(
        a_st=V((2, deepest, count * UR)), b_st=V((2, 2, deepest, unit)), st_sem=dma((2, count + 2)),
        own=V((RING, count, UR, unit), fl), snd_c=block_ring, rcv_c=block_ring,
        zsum=V((ZRING, UR, unit), fl), z_snd=z_ring, z_acc=z_ring, z_mid=z_ring, total=z_ring,
        c_send=dma((CRING,)), c_recv=dma((CRING,)), zi_send=dma((ZRING,)), za_recv=dma((ZRING,)), zm_recv=dma((ZRING,)),
        loc_sem=dma((ZRING,)), mt_send=dma((ORING,)), mt_recv=dma((ORING,)), zo_send=dma((ORING,)), zo_recv=dma((ORING,)),
        d_send=dma((len(bits), 2, RING)), d_recv=dma((len(bits), 2, RING)),
        s_pair=V((rows, width), fl), s_both=V((rows, width), fl), s_plane=V((count, rows, width // count), fl),
        s_line=V((depth, rows, width // count), fl), s_send=dma((count + depth,)), s_recv=dma((count + depth,)),
        load_sem=dma((14,)), store_sem=dma((6,)), small_buf=V((rows, width), fl), sums=V((8, width), fl),
        w_vm=V((inner, width)), w_sem=dma((inner // SLICE,)), up_st=V((2, width, SLICE)), up_sem=dma((2,)),
        in_st=V((2, span, SLICE)), in_sem=dma((2,)), ig_st=V((2, span, SLICE)), ig_sem=dma((2,)),
        grad=V((span, width), fl), acc=V((span, width), fl), x=V((span, width), fl), og=V((span, width)),
        lifted_vm=V((span, 2 * width)), lg_vm=V((span, 2 * width)), padded=V((span + 16, COLS), fl), gated=V((span + 16, COLS), fl),
        vec=vec, pair=pair, plane=plane, line=line, sum_send=dma((count + depth,)), sum_recv=dma((count + depth,)),
        head_st=V((2, 4, span, size)), place_st=V((2, table.shape[0], size)), probs_st=V((2, span, span)), head_sem=dma((2, 6)),
        turned_st=V((2, table.shape[0], size)), turned_sem=dma((2,)), joint_vm=V((span, 3 * width)), mg_vm=V((span, width)),
        turn=V((span, span)))
    tiny = V((8, 128))
    rings = [V((RING, 2, count // 2 ** (j + 1), UR // 2, unit)) if j < len(bits) else tiny for j in range(3)]
    scratch.update(d_snd0=rings[0], d_snd1=rings[1], d_snd2=rings[2], d_rcv0=rings[0], d_rcv1=rings[1], d_rcv2=rings[2])
    names = [["length"] + list(near) + list(far), list(far_outs) + list(near_outs), list(scratch)]
    values = pl.pallas_call(
        functools.partial(backward_kernel, count, depth, heads, shapes, *names),
        out_shape=list(far_outs.values()) + list(near_outs.values()),
        in_specs=[smem] + [vmem] * len(near) + [any_] * len(far),
        out_specs=[any_] * len(far_outs) + [vmem] * len(near_outs),
        scratch_shapes=list(scratch.values()),
        compiler_params=pltpu.CompilerParams(collective_id=collective_id, has_side_effects=True, vmem_limit_bytes=63 * 2**20 + 2**19),
        name="backward",
    )(lengths, *near.values(), *far.values())
    return values[0], values[1], values[-1], [s[:2] for s in shapes]


HEADS = 8


def position_table(span, width):
    distance = (span - 1 - np.arange(2 * span - 1)).astype(np.float32)
    rate = np.exp(np.arange(width // 2).astype(np.float32) * np.float32(-2.0 * math.log(10000.0) / width))
    angle = distance[:, None] * rate[None, :]
    table = np.concatenate([np.sin(angle), np.cos(angle)], axis=1)
    return np.concatenate([table, np.zeros((1, width), np.float32)]).astype(jnp.bfloat16)


def body(count, depth, frames, lengths, cotangent, early_up, early_down, heads_in, offset_proj, heads_out,
         pointwise_up, pointwise_down, late_up, late_down, depthwise, norm_gains, norm_shifts, score_bias):
    _, span, width = frames.shape
    taps = depthwise.shape[0]
    table = jnp.asarray(position_table(span, width))
    small = jnp.concatenate([norm_gains, norm_shifts, score_bias, depthwise], axis=0)
    rows = small.shape[0]
    small = jnp.pad(small, ((0, 32 - rows), (0, 0)))
    wholes, f = forward(count, depth, HEADS, frames[0], cotangent[0], lengths,
                [early_up, early_down, heads_in, offset_proj, heads_out, pointwise_up, pointwise_down, late_up, late_down],
                small, table)
    packed, frames_grad, small_sum, shapes = backward(count, depth, HEADS, frames[0], lengths, wholes, f, table)
    (late_down_grad, late_up_grad, pointwise_down_grad, pointwise_up_grad, heads_out_grad, offset_proj_grad, heads_in_grad,
     early_down_grad, early_up_grad) = unpack(packed, count, shapes)
    return (
        f.output[None], frames_grad[None], early_up_grad, early_down_grad, heads_in_grad, offset_proj_grad, heads_out_grad,
        pointwise_up_grad, pointwise_down_grad, late_up_grad, late_down_grad,
        small_sum[14 : 14 + taps], small_sum[0:6], small_sum[6:12], small_sum[12:14],
    )


def solution(mesh):
    item = P(("dp", "fsdp"), None, None)
    rows = P("fsdp", None)
    cols = P(None, "fsdp")
    in_specs = (item, P(("dp", "fsdp")), item) + (rows,) * 9 + (cols,) * 4
    out_specs = (item, item) + (rows,) * 9 + (cols,) * 4
    count, depth = mesh.shape["fsdp"], mesh.shape["dp"] // 2
    return jax.shard_map(functools.partial(body, count, depth), mesh=mesh, in_specs=in_specs, out_specs=out_specs, check_vma=False)
```

time: 1720 us -> 493 us (0.29)
  waiting for transfers between devices: 1060 us -> 0 us
  Pallas kernels: 0 us -> 482 us
  matrix products: 238 us -> 0 us
  local copies, waits for them, and re-layouts: 212 us -> 7.25 us
  blocking collectives: 119 us -> 0 us
  other arithmetic: 62.6 us -> 1.36 us
    reduce_scatter x10 -> x0, waiting for transfers between devices: 497 us -> none  [the longest x5 252 us: reduce_pair(): lax.psum_scatter(second.astype(jnp.bfloat16), 'fsdp', scatter_dimension=0...]
    pallas_call x0 -> x3, Pallas kernels: none -> 482 us  [the longest x1 266 us: backward(): pl.pallas_call(functools.partial(backward_kernel, count, depth, heads, sh...]
    all_gather x9 -> x0, waiting for transfers between devices: 328 us -> none  [the longest x5 219 us: fetch(): lax.all_gather(second, 'fsdp', axis=0, tiled=True)]
    dot_general x35 -> x0, matrix products: 238 us -> none  [the longest x9 70.9 us: product(): return jnp.dot(left, right, preferred_element_type=jnp.float32)]
    psum x1 -> x0, waiting for transfers between devices: 231 us -> none  [reduce_pair(): lax.psum(shards[1].astype(jnp.bfloat16), 'dp').astype(jnp.float32)]
    psum x3 -> x0, blocking collectives: 108 us -> none  [the longest x1 39.9 us: body(): lax.psum((local[0], local[1], local[2]), ('dp', 'fsdp'))]
    unnamed x262 -> x6, local copies, waits for them, and re-layouts: 103 us -> 3.27 us
    reshape x12 -> x0, local copies, waits for them, and re-layouts: 50.3 us -> none  [the longest x1 17.4 us: rel_shift(): return flat.reshape(lead + (span, 2 * span - 1))[..., :span]]
  transfers between devices with their start and end apart: 20 -> 0, of which waited for: 14 -> 0; matrix products, arithmetic and copies ran while one was open for 19% -> 0% of each run, Pallas kernels for 0% -> 0%
where the time goes in v1:
time: 493 us; the launch traced here: 492 us
  Pallas kernels  482 us (98%)
  local copies, waits for them, and re-layouts  7.25 us (1%)
    pallas_call x1, Pallas kernels, backward(): pl.pallas_call(functools.partial(backward_kernel, count, depth, heads, sh...  266 us
    pallas_call x1, Pallas kernels, forward(): pl.pallas_call(functools.partial(forward_kernel, count, depth, heads, sha...  203 us
    pallas_call x1, Pallas kernels, unpack(): pl.pallas_call(functools.partial(unpack_kernel, tiles), out_shape=out_sha...  12.3 us

profile of v1, /device:TPU:0, one launch (start us, length us, event | category | flops | bytes accessed | tf_op | source)
XLA Modules:
  0.0 492.1 jit_solution(10313146703909741631)
XLA Ops:
  1.3 1.4 fusion.6.refs_4_
  2.6 203.4 %forward.1 = (bf16[1024,4096]{1,0:T(8,128)(2,1)}, bf16[4096,1024]{1,0:T(8,128)(2,1)}, bf16[1024,3072]{1,0:T(8,128)(2,1)}, bf16[1024,1024]{1,0:T(8,128)(2,1)}, bf...) custom-call(s32[1]{0:T(128)S(6)} %copy.34.refs_0_, ...), custom_call_target="tpu_custom_call" | custom-call | tf_op jit(solution)/shard_map/forward/pallas_call | solution.py:664
  206.0 266.5 %backward.1 = (bf16[2,48,128,512]{3,2,1,0:T(8,128)(2,1)}, f32[512,1024]{1,0:T(8,128)}, bf16[512,4096]{1,0:T(8,128)(2,1)}, bf16[512,1024]{1,0:T(8,128)(2,1)}, bf1...) custom-call(s32[1]{0:T(128)S(6)} %copy.34.refs_0_, ...), custom_call_target="tpu_custom_call" | custom-call | tf_op jit(solution)/shard_map/backward/pallas_call | solution.py:1391
  472.5 1.3 slice.15
  473.8 1.3 slice.12
  475.1 1.4 fusion.7
  476.5 0.0 copy-start.1
  476.5 12.3 %unpack_gradients.1 = (f32[1024,1024]{1,0:T(8,128)}, f32[256,4096]{1,0:T(8,128)}, f32[256,1024]{1,0:T(8,128)}, f32[256,2048]{1,0:T(8,128)}, f32[256,1024]{1,0:T(...) custom-call(bf16[2,48,128,512]{3,2,1,0:T(8,128)(2,1)} %get-tuple-element.98.packed), custom_call_target="tpu_custom_call" | custom-call | tf_op jit(solution)/shard_map/unpack_gradients/pallas_call | solution.py:110
  488.8 0.0 copy-start
  488.8 0.0 copy-done.1
  488.8 1.0 copy.35
  489.8 1.0 copy-done
  490.8 1.3 copy.36
Async XLA Ops:
  476.5 12.3 %copy-start.1 = (bf16[512,1024]{1,0:T(8,128)(2,1)S(1)}, bf16[512,1024]{1,0:T(8,128)(2,1)}, u32[]{:S(2)}) copy-start(bf16[512,1024]{1,0:T(8,128)(2,1)} %get-tuple-element.62) | copy-start | bytes 3145732
  488.8 2.0 copy-start

commit v2 on v1

--- a/solution.py
+++ b/solution.py
@@ -45,8 +45,7 @@
     items = []
     for w, (rows, cols) in enumerate(shapes):
         half = rows // 2
-        row_step = min(half, 128 if w == len(shapes) - 1 else 256)
-        col_step = cols if cols <= 2048 else (2048 if cols % 2048 == 0 else 1536)
+        row_step, col_step = min(half, 128), min(cols, 1024)
         for row in range(0, half, row_step):
             for col in range(0, cols, col_step):
                 tiles = col_step // 128
@@ -54,6 +53,9 @@
                 if tiles % 3 == 2 and len(items) % 2:
                     side += 1
                 items.append((w, row, row_step, col, side * 128, (tiles - 2 * side) * 128))
+    for k in (1, 2):
+        w, row, rows, col, edge, middle = items[-k]
+        items[-k] = (w, row, rows, col, 0, middle + 2 * edge)
     return items
 
 
@@ -74,17 +76,18 @@
     return lax.dot_general(left, right, (((0,), (0,)), ((), ())), preferred_element_type=jnp.float32)
 
 
-def unpack_kernel(tiles, packed, *refs):
-    wide_cols = packed.shape[3]
-    many = len(tiles)
-    outs, (held, load, store) = refs[:many], refs[2 * many :]
-    wide = refs[many : 2 * many]
+def unpack_kernel(tiles, cuts, packed, small, *refs):
+    many, unit = len(tiles), packed.shape[3]
+    outs, pieces = refs[:many], refs[many : many + len(cuts)]
+    wide, (held, load, store) = refs[many + len(cuts) : 2 * many + len(cuts)], refs[2 * many + len(cuts) :]
     copies, base = [], 0
     for w, (nr, nc) in enumerate(tiles):
         copy = pltpu.make_async_copy(packed.at[:, pl.ds(base, nr * nc)], held.at[:, pl.ds(base, nr * nc)], load.at[w])
         copy.start()
         copies.append(copy)
         base += nr * nc
+    for piece, (start, stop) in zip(pieces, cuts):
+        piece[...] = small[start:stop]
     base, stores = 0, []
     for w, (nr, nc) in enumerate(tiles):
         copies[w].wait()
@@ -92,7 +95,7 @@
             for col in range(nc):
                 @pl.loop(0, nr)
                 def _(row, w=w, core=core, col=col, base=base, nc=nc):
-                    wide[w][pl.ds(pl.multiple_of(row * UR, UR), UR), (core * nc + col) * wide_cols : (core * nc + col + 1) * wide_cols] = (
+                    wide[w][pl.ds(pl.multiple_of(row * UR, UR), UR), (core * nc + col) * unit : (core * nc + col + 1) * unit] = (
                         held[core, base + row * nc + col].astype(jnp.float32))
         copy = pltpu.make_async_copy(wide[w], outs[w], store.at[w])
         copy.start()
@@ -102,20 +105,22 @@
         copy.wait()
 
 
-def unpack(packed, count, shapes):
-    any_ = pl.BlockSpec(memory_space=pl.ANY)
+def unpack(packed, small, cuts, count, shapes):
+    any_, vmem = pl.BlockSpec(memory_space=pl.ANY), pl.BlockSpec(memory_space=pltpu.VMEM)
     out_shape = [jax.ShapeDtypeStruct((r // count, c), jnp.float32) for r, c in shapes]
+    pieces = [jax.ShapeDtypeStruct((stop - start, small.shape[1]), jnp.float32) for start, stop in cuts]
     tiles = [(r // count // UR, c // 2 // packed.shape[3]) for r, c in shapes]
     dma = pltpu.SemaphoreType.DMA((len(shapes),))
-    return pl.pallas_call(
-        functools.partial(unpack_kernel, tiles),
-        out_shape=out_shape,
-        in_specs=[any_],
-        out_specs=[any_] * len(shapes),
+    values = pl.pallas_call(
+        functools.partial(unpack_kernel, tiles, cuts),
+        out_shape=out_shape + pieces,
+        in_specs=[any_, vmem],
+        out_specs=[any_] * len(shapes) + [vmem] * len(cuts),
         scratch_shapes=[pltpu.VMEM(s.shape, s.dtype) for s in out_shape] + [pltpu.VMEM(packed.shape, packed.dtype), dma, dma],
         compiler_params=pltpu.CompilerParams(vmem_limit_bytes=60 * 2**20),
         name="unpack_gradients",
-    )(packed)
+    )(packed, small)
+    return values[: len(shapes)], values[len(shapes) :]
 
 
 def dot_nn(left, right):
@@ -145,8 +150,8 @@
 
 
 CHUNK = 512
-LEAD = 1
-BUDGET = 9.0
+LEAD, HOP, FAR = 2, 2, 3
+BUDGET = 3.0
 
 
 def forward_kernel(count, depth, heads, shapes, items, saved_names, in_names, out_names, scratch_names, *refs):
@@ -235,17 +240,21 @@
 
     total = len(items)
 
+    place_of = [HOP * step for step in range(steps + 1)]
+    beyond = place_of[-1] + FAR
+    ticks = total + beyond + 2
+
     def gather_tick(tick):
         t = tick + LEAD
         if t < total and tick >= 0:
             plane_send(t, 0)
         for step in range(1, steps):
-            t = tick - step
+            t = tick - place_of[step]
             if 0 <= t < total:
                 wait(recv, t, 2 * step - 2)
                 wait(recv, t, 2 * step - 1)
                 plane_send(t, step)
-        t = tick - steps
+        t = tick - place_of[steps]
         if 0 <= t < total:
             wait(recv, t, 2 * steps - 2)
             wait(recv, t, 2 * steps - 1)
@@ -253,12 +262,12 @@
             if edge:
                 several(t, given, 2 * steps, (twin, me))
             several(t, plane, 2 * steps + 1, (mate, me))
-        t = tick - steps - 1
+        t = tick - beyond
         if 0 <= t < total:
             wait(recv, t, 2 * steps)
             if parts(t)[6]:
                 several(t, parts(t)[5], 2 * steps + 2, (mate, me))
-        t = tick - steps - 2
+        t = tick - beyond - 1
         if 0 <= t < total:
             wait(recv, t, 2 * steps + 1)
             wait(recv, t, 2 * steps + 2)
@@ -608,7 +617,7 @@
     for t in range(min(LEAD, total)):
         plane_send(t, 0)
     done = -1
-    for tick in range(total + steps + 3):
+    for tick in range(ticks):
         finished = gather_tick(tick)
         done = max(done, -1 if finished is None else finished)
         take_arrivals()
@@ -829,7 +838,13 @@
             if half == 1:
                 zm_copy(u).start()
             else:
+                zi_room(u)
                 zi_copy(u).start()
+
+    def zi_room(u):
+        @pl.when(u >= ZRING)
+        def _():
+            pl.semaphore_wait(r.z_free, 1)
 
     def climb(j, u):
         z = lax.rem(u, ZRING)
@@ -842,9 +857,14 @@
         def _():
             zi_copy(u).wait_recv()
             r.z_snd[z] = (r.zsum[z] + r.z_acc[z].astype(jnp.float32)).astype(jnp.bfloat16)
+
+            @pl.when(u < whole - ZRING)
+            def _():
+                pl.semaphore_signal(r.z_free, inc=1, device_id=(outward, me), device_id_type=MESH)
             if j == half - 1:
                 zm_copy(u).start()
             else:
+                zi_room(u)
                 zi_copy(u).start()
 
     def middle(u):
@@ -1156,13 +1176,15 @@
             cond = functools.reduce(jnp.logical_or, [tick == t for t in ticks])
             return pl.when(cond)
 
-        late = tick < 4
-
-        @pl.when(jnp.logical_or(late, jnp.logical_and(tick >= 24, tick < 28)))
-        def _():
-            begin = 2 * jnp.where(late, tick, tick - 24)
-
-            @pl.loop(0, 2)
+        late, begin_late = tick < 6, jnp.where(tick < 2, 2 * tick, tick + 2)
+        several_late = tick < 2
+        tick = tick - 2
+
+        @pl.when(jnp.logical_or(late, jnp.logical_and(tick >= 24, tick < 24 + slices)))
+        def _():
+            begin = jnp.where(late, begin_late, tick - 24)
+
+            @pl.loop(0, jnp.where(several_late, 2, 1))
             def _(k):
                 slice_work(begin + k, late)
 
@@ -1172,7 +1194,7 @@
             for copy in conv_loads[2:]:
                 copy.start()
 
-        @when(31)
+        @when(32)
         def _():
             r.x[...] = r.frames[...].astype(jnp.float32)
             slices_over(r.inner_grad1)
@@ -1258,15 +1280,15 @@
         @when(13 + heads - 1)
         def _():
             joint_store.start()
-
-        when(19)(grad2_store.wait)
-        when(29)(branch_store.wait)
-        joint_parts = [(r.joint_vm, n, n) for n in range(3)]
-
-        @when(21)
-        def _():
             for h in range(2):
                 offsets_store(h).wait()
+
+        when(16)(grad2_store.wait)
+        when(27)(branch_store.wait)
+        joint_parts = [(r.joint_vm, n, n) for n in range(3)]
+
+        @when(21)
+        def _():
             for copy in query_loads:
                 copy.wait()
             older_load.wait()
@@ -1276,9 +1298,10 @@
             begin = (width // COLS // 2) * (tick - 21)
             hidden_cols(begin, begin + width // COLS // 2, joint_parts)
 
+        when(22)(joint_store.wait)
+
         @when(23)
         def _():
-            joint_store.wait()
             branch_store.start()
             r.acc[...] = jnp.zeros_like(r.acc)
             slices_begin(r.early_down, r.early_up, r.inner1)
@@ -1370,7 +1393,7 @@
         a_st=V((2, deepest, count * UR)), b_st=V((2, 2, deepest, unit)), st_sem=dma((2, count + 2)),
         own=V((RING, count, UR, unit), fl), snd_c=block_ring, rcv_c=block_ring,
         zsum=V((ZRING, UR, unit), fl), z_snd=z_ring, z_acc=z_ring, z_mid=z_ring, total=z_ring,
-        c_send=dma((CRING,)), c_recv=dma((CRING,)), zi_send=dma((ZRING,)), za_recv=dma((ZRING,)), zm_recv=dma((ZRING,)),
+        c_send=dma((CRING,)), c_recv=dma((CRING,)), zi_send=dma((ZRING,)), za_recv=dma((ZRING,)), zm_recv=dma((ZRING,)), z_free=pltpu.SemaphoreType.REGULAR,
         loc_sem=dma((ZRING,)), mt_send=dma((ORING,)), mt_recv=dma((ORING,)), zo_send=dma((ORING,)), zo_recv=dma((ORING,)),
         d_send=dma((len(bits), 2, RING)), d_recv=dma((len(bits), 2, RING)),
         s_pair=V((rows, width), fl), s_both=V((rows, width), fl), s_plane=V((count, rows, width // count), fl),
@@ -1423,12 +1446,12 @@
                 [early_up, early_down, heads_in, offset_proj, heads_out, pointwise_up, pointwise_down, late_up, late_down],
                 small, table)
     packed, frames_grad, small_sum, shapes = backward(count, depth, HEADS, frames[0], lengths, wholes, f, table)
+    grads, pieces = unpack(packed, small_sum, [(14, 14 + taps), (0, 6), (6, 12), (12, 14)], count, shapes)
     (late_down_grad, late_up_grad, pointwise_down_grad, pointwise_up_grad, heads_out_grad, offset_proj_grad, heads_in_grad,
-     early_down_grad, early_up_grad) = unpack(packed, count, shapes)
+     early_down_grad, early_up_grad) = grads
     return (
         f.output[None], frames_grad[None], early_up_grad, early_down_grad, heads_in_grad, offset_proj_grad, heads_out_grad,
-        pointwise_up_grad, pointwise_down_grad, late_up_grad, late_down_grad,
-        small_sum[14 : 14 + taps], small_sum[0:6], small_sum[6:12], small_sum[12:14],
+        pointwise_up_grad, pointwise_down_grad, late_up_grad, late_down_grad, *pieces,
     )
 
 

time: 493 us -> 463 us (0.939)
  Pallas kernels: 482 us -> 456 us
    pallas_call x1, Pallas kernels: 203 us -> 187 us  [forward(): pl.pallas_call(functools.partial(forward_kernel, count, depth, heads, sha...]
    pallas_call x1, Pallas kernels: 266 us -> 256 us  [backward(): pl.pallas_call(functools.partial(backward_kernel, count, depth, heads, sh...]
where the time goes in v2:
time: 463 us; the launch traced here: 462 us
  Pallas kernels  456 us (98%)
    pallas_call x1, Pallas kernels, backward(): pl.pallas_call(functools.partial(backward_kernel, count, depth, heads, sh...  256 us
    pallas_call x1, Pallas kernels, forward(): pl.pallas_call(functools.partial(forward_kernel, count, depth, heads, sha...  187 us
    pallas_call x1, Pallas kernels, unpack(): pl.pallas_call(functools.partial(unpack_kernel, tiles, cuts), out_shape=o...  13.4 us

profile of v2, /device:TPU:0, one launch (start us, length us, event | category | flops | bytes accessed | tf_op | source)
XLA Modules:
  0.0 462.4 jit_solution(5544162860809314468)
XLA Ops:
  1.3 1.4 fusion.6.refs_4_
  2.6 186.6 %forward.1 = (bf16[1024,4096]{1,0:T(8,128)(2,1)}, bf16[4096,1024]{1,0:T(8,128)(2,1)}, bf16[1024,3072]{1,0:T(8,128)(2,1)}, bf16[1024,1024]{1,0:T(8,128)(2,1)}, bf...) custom-call(s32[1]{0:T(128)S(6)} %copy.34.refs_0_, ...), custom_call_target="tpu_custom_call" | custom-call | tf_op jit(solution)/shard_map/forward/pallas_call | solution.py:673
  189.3 256.5 %backward.1 = (bf16[2,48,128,512]{3,2,1,0:T(8,128)(2,1)}, f32[512,1024]{1,0:T(8,128)}, bf16[512,4096]{1,0:T(8,128)(2,1)}, bf16[512,1024]{1,0:T(8,128)(2,1)}, bf1...) custom-call(s32[1]{0:T(128)S(6)} %copy.34.refs_0_, ...), custom_call_target="tpu_custom_call" | custom-call | tf_op jit(solution)/shard_map/backward/pallas_call | solution.py:1414
  445.7 0.0 copy-start.1
  445.8 13.4 %unpack_gradients.1 = (f32[1024,1024]{1,0:T(8,128)}, f32[256,4096]{1,0:T(8,128)}, f32[256,1024]{1,0:T(8,128)}, f32[256,2048]{1,0:T(8,128)}, f32[256,1024]{1,0:T(...) custom-call(bf16[2,48,128,512]{3,2,1,0:T(8,128)(2,1)} %get-tuple-ele, ...), custom_call_target="tpu_custom_call" | custom-call | tf_op jit(solution)/shard_map/unpack_gradients/pallas_call | solution.py:114
  459.1 0.0 copy-start
  459.1 0.0 copy-done.1
  459.1 1.0 copy.35
  460.1 1.0 copy-done
  461.1 1.3 copy.36
Async XLA Ops:
  445.7 13.4 %copy-start.1 = (bf16[512,1024]{1,0:T(8,128)(2,1)S(1)}, bf16[512,1024]{1,0:T(8,128)(2,1)}, u32[]{:S(2)}) copy-start(bf16[512,1024]{1,0:T(8,128)(2,1)} %get-tuple-element.66) | copy-start | bytes 3145732
  459.1 2.0 copy-start

commit v3 on v2

--- a/solution.py
+++ b/solution.py
@@ -150,7 +150,7 @@
 
 
 CHUNK = 512
-LEAD, HOP, FAR = 2, 2, 3
+LEAD, HOP, FAR = 2, 2, 2
 BUDGET = 3.0
 
 
@@ -1191,6 +1191,8 @@
         @when(4)
         def _():
             slices_over(r.inner_grad4)
+            starts[0].wait()
+            starts[1].wait()
             for copy in conv_loads[2:]:
                 copy.start()
 
@@ -1326,10 +1328,11 @@
     for device in line_to:
         pl.semaphore_signal(barrier, inc=1, device_id=device, device_id_type=MESH)
     starts = [loading(r.grad4, r.grad, 0), loading(r.x3, r.x, 1), loading(r.branch4, r.og, 13)]
-    for copy in starts:
-        copy.start()
     fetch_unit(jnp.int32(0))
+    starts[2].start()
     slices_begin(r.late_down, r.late_up, r.inner4)
+    starts[0].start()
+    starts[1].start()
     r.acc[...] = jnp.zeros_like(r.acc)
     r.small_buf[...] = jnp.zeros_like(r.small_buf)
     r.small_buf[4:5] = r.edge_grads[0:1]
@@ -1342,8 +1345,7 @@
     column = lax.broadcasted_iota(jnp.int32, (span, span), 1)
     r.turn[...] = jnp.where(row + column == span - 1, 1.0, 0.0).astype(jnp.bfloat16)
     pl.semaphore_wait(barrier, 1 + count - 1 + depth - 1)
-    for copy in starts:
-        copy.wait()
+    starts[2].wait()
 
     @pl.loop(0, whole + at + 1)
     def _(tick):

time: 463 us -> 463 us (level)
  no operation moved by 1% of the time
where the time goes in v3:
time: 463 us; the launch traced here: 462 us
  Pallas kernels  456 us (98%)
    pallas_call x1, Pallas kernels, backward(): pl.pallas_call(functools.partial(backward_kernel, count, depth, heads, sh...  255 us
    pallas_call x1, Pallas kernels, forward(): pl.pallas_call(functools.partial(forward_kernel, count, depth, heads, sha...  188 us
    pallas_call x1, Pallas kernels, unpack(): pl.pallas_call(functools.partial(unpack_kernel, tiles, cuts), out_shape=o...  13.4 us

profile of v3, /device:TPU:0, one launch (start us, length us, event | category | flops | bytes accessed | tf_op | source)
XLA Modules:
  0.0 462.5 jit_solution(513645948808218901)
XLA Ops:
  1.3 1.4 fusion.6.refs_4_
  2.6 188.5 %forward.1 = (bf16[1024,4096]{1,0:T(8,128)(2,1)}, bf16[4096,1024]{1,0:T(8,128)(2,1)}, bf16[1024,3072]{1,0:T(8,128)(2,1)}, bf16[1024,1024]{1,0:T(8,128)(2,1)}, bf...) custom-call(s32[1]{0:T(128)S(6)} %copy.34.refs_0_, ...), custom_call_target="tpu_custom_call" | custom-call | tf_op jit(solution)/shard_map/forward/pallas_call | solution.py:673
  191.1 254.7 %backward.1 = (bf16[2,48,128,512]{3,2,1,0:T(8,128)(2,1)}, f32[512,1024]{1,0:T(8,128)}, bf16[512,4096]{1,0:T(8,128)(2,1)}, bf16[512,1024]{1,0:T(8,128)(2,1)}, bf1...) custom-call(s32[1]{0:T(128)S(6)} %copy.34.refs_0_, ...), custom_call_target="tpu_custom_call" | custom-call | tf_op jit(solution)/shard_map/backward/pallas_call | solution.py:1416
  445.8 0.0 copy-start.1
  445.8 13.4 %unpack_gradients.1 = (f32[1024,1024]{1,0:T(8,128)}, f32[256,4096]{1,0:T(8,128)}, f32[256,1024]{1,0:T(8,128)}, f32[256,2048]{1,0:T(8,128)}, f32[256,1024]{1,0:T(...) custom-call(bf16[2,48,128,512]{3,2,1,0:T(8,128)(2,1)} %get-tuple-ele, ...), custom_call_target="tpu_custom_call" | custom-call | tf_op jit(solution)/shard_map/unpack_gradients/pallas_call | solution.py:114
  459.2 0.0 copy-start
  459.2 0.0 copy-done.1
  459.2 1.0 copy.35
  460.2 1.0 copy-done
  461.1 1.3 copy.36
Async XLA Ops:
  445.8 13.4 %copy-start.1 = (bf16[512,1024]{1,0:T(8,128)(2,1)S(1)}, bf16[512,1024]{1,0:T(8,128)(2,1)}, u32[]{:S(2)}) copy-start(bf16[512,1024]{1,0:T(8,128)(2,1)} %get-tuple-element.66) | copy-start | bytes 3145732
  459.2 2.0 copy-start
